TPU v7x, 32 devices: a whole 2x2x4 slice. The times are simulated.
32 devices in a mesh: dp: 2 (over x), expert: 16 (over z, y, core).
Axes of the slice: x: 2, y: 2, z: 4, core: 2. Of those that a mesh axis runs over, the one named last changes fastest.
Arguments:
- tokens: bfloat16 [8192, 1536], P(('dp', 'expert')), may hold values from -6 to 6
- cotangent: bfloat16 [8192, 1536], P(('dp', 'expert')), may hold values from -6 to 6
- lengths: int32 [32], P(('dp', 'expert')), may hold values from 64 to 256, as said below
- routes: int32 [8192, 8], P(('dp', 'expert')), may hold values from 0 to 15, all different within a row; in each aligned block of 256 rows (0 to 255, 256 to 511, ...) at most 160 rows name the same one
- norm1_gain: bfloat16 [1536], P('expert'), may hold values from 0.5 to 1.5
- w_query: bfloat16 [1536, 1536], P('expert'), may hold values from -0.15625 to 0.15625
- w_kv: bfloat16 [1536, 1024], P('expert'), may hold values from -0.15625 to 0.15625
- w_out: bfloat16 [1536, 1536], P('expert'), may hold values from -0.625 to 0.625
- norm2_gain: bfloat16 [1536], P('expert'), may hold values from 0.5 to 1.5
- w_router: bfloat16 [1536, 16], P('expert'), may hold values from -0.078125 to 0.078125
- expert_gate: bfloat16 [16, 1536, 512], P('expert'), may hold values from -0.15625 to 0.15625
- expert_up: bfloat16 [16, 1536, 512], P('expert'), may hold values from -0.15625 to 0.15625
- expert_down: bfloat16 [16, 512, 1536], P('expert'), may hold values from -1 to 1
Outputs:
- output: bfloat16 [8192, 1536], P(('dp', 'expert'))
- input_grad: bfloat16 [8192, 1536], P(('dp', 'expert'))
- grad_norm1_gain: float32 [1536], P('expert')
- grad_w_query: float32 [1536, 1536], P('expert')
- grad_w_kv: float32 [1536, 1024], P('expert')
- grad_w_out: float32 [1536, 1536], P('expert')
- grad_norm2_gain: float32 [1536], P('expert')
- grad_w_router: float32 [1536, 16], P('expert')
- grad_expert_gate: float32 [16, 1536, 512], P('expert')
- grad_expert_up: float32 [16, 1536, 512], P('expert')
- grad_expert_down: float32 [16, 512, 1536], P('expert')
Inputs may be any that keep to these rules, and one draw needn't show every extreme that they name: `routes`: each row names 8 different experts; among the rows of one device no expert is named more than 160 times. `lengths`: one sequence a device, holding that device's 256 rows of tokens; slots at or past its length are padding.
All inputs are finite; a program needn't handle non-finite values.
Results may differ from a plain program's by a relative error of at most 0.024.
Values may be sent and summed in bfloat16 or wider, within the bound.
A program may use at most 192 MiB of HBM per device.

v0:
```python
import jax
import jax.numpy as jnp
from jax import lax
from jax.sharding import PartitionSpec as P

HD = 64


EPSILON = 1e-05


def rotate(values, cosine, sines):
    half_dim = values.shape[-1] // 2
    first_half = values[..., :half_dim]
    second_half = values[..., half_dim:]
    return jnp.concatenate(
        [first_half * cosine - second_half * sines, second_half * cosine + first_half * sines], -1
    )


def rotate_back(grads, cosine, sines):
    half_dim = grads.shape[-1] // 2
    first_half = grads[..., :half_dim]
    second_half = grads[..., half_dim:]
    return jnp.concatenate(
        [first_half * cosine + second_half * sines, second_half * cosine - first_half * sines], -1
    )


def rope_tables(length, head_dim):
    half_dim = head_dim // 2
    positions = jnp.arange(length).astype(jnp.float32)
    inverse = jnp.power(jnp.float32(10000.0), -jnp.arange(half_dim).astype(jnp.float32) / half_dim)
    angles = positions[:, None] * inverse[None, :]
    return (jnp.cos(angles)[:, None, :], jnp.sin(angles)[:, None, :])


def norm_back(grad_normed, values, inverse, gain):
    scaled = grad_normed * gain
    gain_grad = jnp.sum(grad_normed * values * inverse, axis=0)
    value_grad = inverse * scaled - values * inverse * inverse * inverse * jnp.mean(
        scaled * values, axis=-1, keepdims=True
    )
    return (gain_grad, value_grad)


def per_device(
    tokens,
    cotangent,
    lengths,
    routes,
    norm1_gain,
    w_query,
    w_kv,
    w_out,
    norm2_gain,
    w_router,
    expert_gate,
    expert_up,
    expert_down,
):
    tok_rows, model_width = tokens.shape
    top_count = routes.shape[1]
    expert_count = w_router.shape[1]
    group_size = lax.axis_size("expert")
    capacity = min(tok_rows, 5 * tok_rows * top_count // (4 * expert_count))
    head_dim = HD
    kv_count = w_kv.shape[1] // (2 * head_dim)
    head_count = w_query.shape[1] // head_dim
    per_group = head_count // kv_count
    score_scale = head_dim ** (-0.5)
    f32 = jnp.float32
    bf16 = jnp.bfloat16
    gathered = (
        lax.all_gather(norm1_gain, "expert", axis=0, tiled=True),
        lax.all_gather(norm2_gain, "expert", axis=0, tiled=True),
        lax.all_gather(w_query, "expert", axis=0, tiled=True),
        lax.all_gather(w_kv, "expert", axis=0, tiled=True),
        lax.all_gather(w_out, "expert", axis=0, tiled=True),
        lax.all_gather(w_router, "expert", axis=0, tiled=True),
    )
    gain_one = gathered[0].astype(f32)
    gain_two = gathered[1].astype(f32)
    query_w, kv_w, out_w, router_w = (gathered[2], gathered[3], gathered[4], gathered[5])
    inputs = tokens.astype(f32)
    inv_one = lax.rsqrt(jnp.mean(inputs * inputs, axis=-1, keepdims=True) + EPSILON)
    normed_one = (inputs * inv_one * gain_one).astype(bf16)
    query_proj = jnp.dot(normed_one, query_w, preferred_element_type=f32)
    kv_proj = jnp.dot(normed_one, kv_w, preferred_element_type=f32)
    cosine, sines = rope_tables(tok_rows, head_dim)
    queries = (
        rotate(query_proj.reshape(tok_rows, head_count, head_dim), cosine, sines)
        .astype(bf16)
        .reshape(tok_rows, kv_count, per_group, head_dim)
    )
    keys = rotate(
        kv_proj[:, : kv_count * head_dim].reshape(tok_rows, kv_count, head_dim), cosine, sines
    ).astype(bf16)
    values = kv_proj[:, kv_count * head_dim :].reshape(tok_rows, kv_count, head_dim).astype(bf16)
    causal = jnp.arange(tok_rows)[:, None] >= jnp.arange(tok_rows)[None, :]

    def masked_scores():
        scores = (
            jnp.einsum("tgjd,ugd->gjtu", queries, keys, preferred_element_type=f32) * score_scale
        )
        return jnp.where(causal[None, None], scores, -1e30)

    masked = masked_scores()
    row_peak = jnp.max(masked, axis=-1, keepdims=True)
    exp_scores = jnp.exp(masked - row_peak)
    row_total = jnp.sum(exp_scores, axis=-1, keepdims=True)
    log_total = row_peak + jnp.log(row_total)
    probs_low = (exp_scores / row_total).astype(bf16)
    attended = (
        jnp.einsum("gjtu,ugd->tgjd", probs_low, values, preferred_element_type=f32)
        .astype(bf16)
        .reshape(tok_rows, head_count * head_dim)
    )
    middle = inputs + jnp.dot(attended, out_w, preferred_element_type=f32)
    inv_two = lax.rsqrt(jnp.mean(middle * middle, axis=-1, keepdims=True) + EPSILON)
    mixed_in = (middle * inv_two * gain_two).astype(bf16)
    logits = jnp.dot(mixed_in, router_w, preferred_element_type=f32)
    chosen = routes[:, :, None] == jnp.arange(expert_count)[None, None, :]
    chosen_float = chosen.astype(f32)
    selected = jnp.sum(chosen_float * logits[:, None, :], axis=-1)
    gates = jax.nn.softmax(selected, axis=-1)
    flat_chosen = chosen.reshape(-1, expert_count).astype(jnp.int32)
    running_count = jnp.cumsum(flat_chosen, axis=0) - 1
    slot_index = jnp.sum(running_count * flat_chosen, axis=-1)
    target = routes.reshape(-1) * capacity + slot_index
    source_token = jnp.arange(tok_rows * top_count) // top_count
    slot_token = jnp.zeros((expert_count * capacity,), jnp.int32).at[target].set(source_token)
    slot_live = jnp.zeros((expert_count * capacity,), jnp.bool_).at[target].set(True)
    slot_gate = jnp.zeros((expert_count * capacity,), f32).at[target].set(gates.reshape(-1))
    outgoing = jnp.where(slot_live[:, None], mixed_in[slot_token], jnp.zeros((), bf16)).reshape(
        expert_count, capacity, model_width
    )
    arrived = lax.all_to_all(outgoing, "expert", split_axis=0, concat_axis=0, tiled=True).reshape(
        -1, model_width
    )
    gate_mat = expert_gate[0]
    up_mat = expert_up[0]
    down_mat = expert_down[0]
    gate_pre = jnp.dot(arrived, gate_mat, preferred_element_type=f32)
    up_pre = jnp.dot(arrived, up_mat, preferred_element_type=f32)
    hidden = (jax.nn.silu(gate_pre) * up_pre).astype(bf16)
    expert_out = jnp.dot(hidden, down_mat, preferred_element_type=f32).astype(bf16)
    returned = lax.all_to_all(
        expert_out.reshape(group_size, capacity, model_width),
        "expert",
        split_axis=0,
        concat_axis=0,
        tiled=True,
    ).reshape(-1, model_width)
    picked = returned[target].reshape(tok_rows, top_count, model_width)
    mixture = jnp.sum(picked.astype(f32) * gates[:, :, None], axis=1)
    output = (middle + mixture).astype(bf16)
    back_gain_one = gathered[0].astype(f32)
    back_gain_two = gathered[1].astype(f32)
    back_query, back_kv, back_out, back_router = (
        gathered[2],
        gathered[3],
        gathered[4],
        gathered[5],
    )
    live = (jnp.arange(tok_rows) < lengths[0]).astype(f32)
    d_out = cotangent.astype(f32) * live[:, None]
    d_gates = jnp.sum(picked.astype(f32) * d_out[:, None, :], axis=-1)
    d_sel = gates * (d_gates - jnp.sum(gates * d_gates, axis=-1, keepdims=True))
    d_logits = jnp.sum(d_sel[:, :, None] * chosen_float, axis=1).astype(bf16)
    grad_router = jnp.dot(mixed_in.T, d_logits, preferred_element_type=f32)
    d_mixed_router = jnp.dot(d_logits, back_router.T, preferred_element_type=f32)
    grad_out_rows = (
        (d_out[slot_token] * slot_gate[:, None])
        .astype(bf16)
        .reshape(expert_count, capacity, model_width)
    )
    grad_arrived = lax.all_to_all(
        grad_out_rows, "expert", split_axis=0, concat_axis=0, tiled=True
    ).reshape(-1, model_width)
    d_hidden = jnp.dot(grad_arrived, down_mat.T, preferred_element_type=f32)
    sigma = jax.nn.sigmoid(gate_pre)
    d_gate_pre = (d_hidden * up_pre * sigma * (1.0 + gate_pre * (1.0 - sigma))).astype(bf16)
    d_up_pre = (d_hidden * gate_pre * sigma).astype(bf16)
    grad_down = jnp.dot(hidden.T, grad_arrived, preferred_element_type=f32)
    grad_gate = jnp.dot(arrived.T, d_gate_pre, preferred_element_type=f32)
    grad_up = jnp.dot(arrived.T, d_up_pre, preferred_element_type=f32)
    d_arrived = (
        jnp.dot(d_gate_pre, gate_mat.T, preferred_element_type=f32)
        + jnp.dot(d_up_pre, up_mat.T, preferred_element_type=f32)
    ).astype(bf16)
    grad_returned = lax.all_to_all(
        d_arrived.reshape(group_size, capacity, model_width),
        "expert",
        split_axis=0,
        concat_axis=0,
        tiled=True,
    ).reshape(-1, model_width)
    d_mixed = (
        jnp.sum(grad_returned[target].reshape(tok_rows, top_count, model_width).astype(f32), axis=1)
        + d_mixed_router
    )
    grad_gain_two, d_middle_norm = norm_back(d_mixed, middle, inv_two, back_gain_two)
    d_middle = d_out + d_middle_norm
    d_middle_low = d_middle.astype(bf16)
    grad_out_w = jnp.dot(attended.T, d_middle_low, preferred_element_type=f32)
    d_attended = (
        jnp.dot(d_middle_low, back_out.T, preferred_element_type=f32)
        .astype(bf16)
        .reshape(tok_rows, kv_count, per_group, head_dim)
    )
    probs_full = jnp.where(causal[None, None], jnp.exp(masked_scores() - log_total), 0.0)
    probs_again = probs_full.astype(bf16)
    d_probs = jnp.einsum("tgjd,ugd->gjtu", d_attended, values, preferred_element_type=f32)
    d_values = jnp.einsum("gjtu,tgjd->ugd", probs_again, d_attended, preferred_element_type=f32)
    d_scores = (
        probs_full * (d_probs - jnp.sum(probs_full * d_probs, axis=-1, keepdims=True))
    ).astype(bf16)
    d_queries = (
        jnp.einsum("gjtu,ugd->tgjd", d_scores, keys, preferred_element_type=f32) * score_scale
    )
    d_keys = (
        jnp.einsum("gjtu,tgjd->ugd", d_scores, queries, preferred_element_type=f32) * score_scale
    )
    d_query_proj = (
        rotate_back(d_queries.reshape(tok_rows, head_count, head_dim), cosine, sines)
        .reshape(tok_rows, -1)
        .astype(bf16)
    )
    d_kv_proj = jnp.concatenate(
        [rotate_back(d_keys, cosine, sines).reshape(tok_rows, -1), d_values.reshape(tok_rows, -1)],
        axis=-1,
    ).astype(bf16)
    grad_query = jnp.dot(normed_one.T, d_query_proj, preferred_element_type=f32)
    grad_kv = jnp.dot(normed_one.T, d_kv_proj, preferred_element_type=f32)
    d_normed = jnp.dot(d_query_proj, back_query.T, preferred_element_type=f32) + jnp.dot(
        d_kv_proj, back_kv.T, preferred_element_type=f32
    )
    grad_gain_one, d_input_norm = norm_back(d_normed, inputs, inv_one, back_gain_one)
    input_grad = (d_middle + d_input_norm).astype(bf16)
    local_shards = (
        lax.psum_scatter(
            grad_gain_one.astype(jnp.bfloat16), "expert", scatter_dimension=0, tiled=True
        ).astype(jnp.float32),
        lax.psum_scatter(
            grad_gain_two.astype(jnp.bfloat16), "expert", scatter_dimension=0, tiled=True
        ).astype(jnp.float32),
        lax.psum_scatter(
            grad_query.astype(jnp.bfloat16), "expert", scatter_dimension=0, tiled=True
        ).astype(jnp.float32),
        lax.psum_scatter(
            grad_kv.astype(jnp.bfloat16), "expert", scatter_dimension=0, tiled=True
        ).astype(jnp.float32),
        lax.psum_scatter(
            grad_out_w.astype(jnp.bfloat16), "expert", scatter_dimension=0, tiled=True
        ).astype(jnp.float32),
        lax.psum_scatter(
            grad_router.astype(jnp.bfloat16), "expert", scatter_dimension=0, tiled=True
        ).astype(jnp.float32),
    )
    summed = (
        lax.psum(local_shards[0].astype(jnp.bfloat16), "dp").astype(jnp.float32),
        lax.psum(local_shards[1].astype(jnp.bfloat16), "dp").astype(jnp.float32),
        lax.psum(local_shards[2].astype(jnp.bfloat16), "dp").astype(jnp.float32),
        lax.psum(local_shards[3].astype(jnp.bfloat16), "dp").astype(jnp.float32),
        lax.psum(local_shards[4].astype(jnp.bfloat16), "dp").astype(jnp.float32),
        lax.psum(local_shards[5].astype(jnp.bfloat16), "dp").astype(jnp.float32),
        lax.psum(grad_gate[None].astype(jnp.bfloat16), "dp").astype(jnp.float32),
        lax.psum(grad_up[None].astype(jnp.bfloat16), "dp").astype(jnp.float32),
        lax.psum(grad_down[None].astype(jnp.bfloat16), "dp").astype(jnp.float32),
    )
    return (
        output,
        input_grad,
        summed[0],
        summed[2],
        summed[3],
        summed[4],
        summed[1],
        summed[5],
        summed[6],
        summed[7],
        summed[8],
    )


def solution(mesh):
    placed = (
        P(("dp", "expert"), None),
        P(("dp", "expert"), None),
        P(("dp", "expert")),
        P(("dp", "expert"), None),
        P("expert"),
        P("expert", None),
        P("expert", None),
        P("expert", None),
        P("expert"),
        P("expert", None),
        P("expert", None, None),
        P("expert", None, None),
        P("expert", None, None),
    )
    return jax.shard_map(
        per_device,
        mesh=mesh,
        in_specs=placed,
        out_specs=(
            P(("dp", "expert"), None),
            P(("dp", "expert"), None),
            P("expert"),
            P("expert", None),
            P("expert", None),
            P("expert", None),
            P("expert"),
            P("expert", None),
            P("expert", None, None),
            P("expert", None, None),
            P("expert", None, None),
        ),
        check_vma=False,
    )
```

profile of v0, /device:TPU:0, one launch (start us, length us, event | category | flops | bytes accessed | tf_op | source)
XLA Modules:
  0.0 1444.5 jit_solution(2809261958114359833)
XLA Ops:
  14.2 36.1 %all-reduce.5 = (bf16[1536]{0:T(1024)(128)(2,1)S(1)}, bf16[1536]{0:T(1024)(128)(2,1)S(1)}) all-reduce(bf16[1536]{0:T(1024)(128)(2,1)S(1)} %dynamic-update-slice, bf16[1536]{0:T(1024)(128)(2,1)S(1)} %dynamic-update-slice.1), channel_id=1, replica_groups=mesh['dp'=2,'expert'=16] {'expert'}, use_global_device_ids=true, to_apply=%add | all-reduce | flops 3072 | bytes 12288
  56.7 9.1 scatter_custom_fusion
  66.5 8.2 scatter_custom_fusion.1
  81.1 31.9 %all-gather.7.cloned.1.call-done = bf16[1536,1536]{1,0:T(8,128)(2,1)} async-done(((bf16[96,1536]{1,0:T(8,128)(2,1)}), bf16[1536,1536]{1,0:T(8,128)(2,1)}) %all-gather.7.cloned.1.call-update) | async-done | bytes 4718608 | tf_op jit(solution)/shard_map/all_gather | solution.py:77
  122.8 44.4 %all-gather.9.cloned.1.call-done = bf16[1536,1536]{1,0:T(8,128)(2,1)} async-done(((bf16[96,1536]{1,0:T(8,128)(2,1)}), bf16[1536,1536]{1,0:T(8,128)(2,1)}) %all-gather.9.cloned.1.call-update) | async-done | bytes 4718608 | tf_op jit(solution)/shard_map/all_gather | solution.py:79
  172.3 9.5 gather_fusion
  194.4 142.7 %all-gather = bf16[16,96,16]{1,2,0:T(8,128)(2,1)S(1)} all-gather(bf16[1,96,16]{1,2,0:T(8,128)(2,1)S(1)} %bitcast.187), channel_id=1, replica_groups=mesh['dp'=2,'expert'=16] {'expert'}, dimensions={0}, use_global_device_ids=true | all-gather | bytes 52224 | tf_op jit(solution)/shard_map/all_gather | solution.py:80
  338.7 10.4 gather_fusion.2
  359.0 8.6 multiply_convert_fusion
  367.6 42.2 %all-to-all-start.2 = ((bf16[16,160,1536]{2,1,0:T(8,128)(2,1)}), bf16[16,160,1536]{2,1,0:T(8,128)(2,1)}, u32[]{:S(2)}, u32[]{:S(2)}) async-start(bf16[16,160,1536]{2,1,0:T(8,128)(2,1)} %multiply_convert_fusion), calls=%async_computation.2 | async-start | bytes 15728640 | tf_op jit(solution)/shard_map/all_to_all | solution.py:178
  409.8 10.4 fusion.32
  420.2 9.2 fusion.36
  429.4 121.9 %all-to-all-done.2 = bf16[16,160,1536]{2,1,0:T(8,128)(2,1)} async-done(((bf16[16,160,1536]{2,1,0:T(8,128)(2,1)}), bf16[16,160,1536]{2,1,0:T(8,128)(2,1)}, u32[]{:S(2)}, u32[]{:S(2)}) %all-to-all-start.2) | async-done | bytes 7864352 | tf_op jit(solution)/shard_map/all_to_all | solution.py:178
  551.4 12.7 multiply_convert_fusion.1
  570.5 35.6 %all-to-all-start.1 = ((bf16[16,160,1536]{2,1,0:T(8,128)(2,1)}), bf16[16,160,1536]{2,1,0:T(8,128)(2,1)}, u32[]{:S(2)}, u32[]{:S(2)}) async-start(bf16[16,160,1536]{2,1,0:T(8,128)(2,1)} %bitcast.162), calls=%async_computation.1 | async-start | bytes 15728640 | tf_op jit(solution)/shard_map/all_to_all | solution.py:148
  606.1 9.7 fusion.34
  615.8 10.0 add_convert_fusion
  625.8 121.8 %all-to-all-done.1 = bf16[16,160,1536]{2,1,0:T(8,128)(2,1)} async-done(((bf16[16,160,1536]{2,1,0:T(8,128)(2,1)}), bf16[16,160,1536]{2,1,0:T(8,128)(2,1)}, u32[]{:S(2)}, u32[]{:S(2)}) %all-to-all-start.1) | async-done | bytes 7864352 | tf_op jit(solution)/shard_map/all_to_all | solution.py:148
  747.6 34.6 %all-to-all-start.3 = ((bf16[16,160,1536]{2,1,0:T(8,128)(2,1)}), bf16[16,160,1536]{2,1,0:T(8,128)(2,1)}, u32[]{:S(2)}, u32[]{:S(2)}) async-start(bf16[16,160,1536]{2,1,0:T(8,128)(2,1)} %bitcast.161), calls=%async_computation.3 | async-start | bytes 15728640 | tf_op jit(solution)/shard_map/all_to_all | solution.py:192
  782.3 17.6 %gather_fusion.1 = bf16[2048,1536]{1,0:T(8,128)(2,1)} fusion(bf16[2560,1536]{1,0:T(8,128)(2,1)} %bitcast.22, s32[2048]{0:T(1024)S(1)} %broadcast_clamp_fusion), kind=kCustom, calls=%fused_computation.1 | custom fusion | bytes 12591104 | tf_op jit(solution)/shard_map/gather | solution.py:155
  799.9 9.5 fusion.1
  809.5 114.3 %all-to-all-done.3 = bf16[16,160,1536]{2,1,0:T(8,128)(2,1)} async-done(((bf16[16,160,1536]{2,1,0:T(8,128)(2,1)}), bf16[16,160,1536]{2,1,0:T(8,128)(2,1)}, u32[]{:S(2)}, u32[]{:S(2)}) %all-to-all-start.3) | async-done | bytes 7864352 | tf_op jit(solution)/shard_map/all_to_all | solution.py:192
  923.8 17.7 %gather_fusion.3 = bf16[2048,1536]{1,0:T(8,128)(2,1)} fusion(bf16[2560,1536]{1,0:T(8,128)(2,1)} %bitcast.29, s32[2048]{0:T(1024)S(1)} %broadcast_clamp_fusion), kind=kCustom, calls=%fused_computation.3 | custom fusion | bytes 12591104 | tf_op jit(solution)/shard_map/gather | solution.py:200
  985.4 9.6 fusion.14
  995.0 8.7 fusion.13
  1005.2 9.7 fusion.15
  1014.8 53.9 %reduce-scatter.9.cloned.1.call-done = bf16[96,1024]{1,0:T(8,128)(2,1)} async-done(((bf16[1536,1024]{1,0:T(8,128)(2,1)}), bf16[96,1024]{1,0:T(8,128)(2,1)}) %reduce-scatter.9.cloned.1.call-update) | async-done | bytes 196624 | tf_op jit(solution)/shard_map/reduce_scatter | solution.py:251
  1068.7 78.3 %reduce-scatter.11.cloned.1.call-done = bf16[96,1536]{1,0:T(8,128)(2,1)} async-done(((bf16[1536,1536]{1,0:T(8,128)(2,1)}), bf16[96,1536]{1,0:T(8,128)(2,1)}) %reduce-scatter.11.cloned.1.call-update) | async-done | bytes 294928 | tf_op jit(solution)/shard_map/reduce_scatter | solution.py:254
  1146.9 78.8 %reduce-scatter.7.cloned.1.call-done = bf16[96,1536]{1,0:T(8,128)(2,1)} async-done(((bf16[1536,1536]{1,0:T(8,128)(2,1)}), bf16[96,1536]{1,0:T(8,128)(2,1)}) %reduce-scatter.7.cloned.1.call-update) | async-done | bytes 294928 | tf_op jit(solution)/shard_map/reduce_scatter | solution.py:248
  1232.8 30.6 %all-reduce.4 = (bf16[1536]{0:T(1024)(128)(2,1)S(1)}, bf16[1536]{0:T(1024)(128)(2,1)S(1)}) all-reduce(bf16[1536]{0:T(1024)(128)(2,1)S(1)} %get-tuple-element.15, bf16[1536]{0:T(1024)(128)(2,1)S(1)} %get-tuple-element.13), channel_id=2, replica_groups=mesh['dp'=2,'expert'=16] {'expert'}, use_global_device_ids=true, to_apply=%region_22.23.clone | all-reduce | flops 3072 | bytes 12288
  1266.5 18.0 %reduce-scatter.13.cloned.1.call-done = bf16[96,16]{1,0:T(8,128)(2,1)} async-done(((bf16[1536,16]{1,0:T(8,128)(2,1)}), bf16[96,16]{1,0:T(8,128)(2,1)}) %reduce-scatter.13.cloned.1.call-update) | async-done | bytes 3088
  1291.9 133.4 %all-reduce.10.cloned.1.call-done = (bf16[96,1536]{1,0:T(8,128)(2,1)}, bf16[96,1024]{1,0:T(8,128)(2,1)}, bf16[96,1536]{1,0:T(8,128)(2,1)}, bf16[1,1536,512]{2,1,...) async-done(((bf16[96,1536]{1,0:T(8,128)(2,1)}, bf16[96,1024]{1,0:T(8,128)(2,1)}, bf16[96,1536]{1,0:T(8,128)(2,1)}, ...) | async-done | bytes 5505040 | tf_op jit(solution)/shard_map/psum | solution.py:264
  (262 shorter events, 137.8 us)
Async XLA Ops:
  7.2 544.2 %copy-start = (bf16[1,512,1536]{2,1,0:T(8,128)(2,1)S(1)}, bf16[1,512,1536]{2,1,0:T(8,128)(2,1)}, u32[]{:S(2)}) copy-start(bf16[1,512,1536]{2,1,0:T(8,128)(2,1)} %param.25) | copy-start | bytes 4718596
  7.2 68.2 %copy-start.5 = (bf16[256,1536]{1,0:T(8,128)(2,1)S(1)}, bf16[256,1536]{1,0:T(8,128)(2,1)}, u32[]{:S(2)}) copy-start(bf16[256,1536]{1,0:T(8,128)(2,1)} %param.13) | copy-start | bytes 2359300
  7.2 68.7 %all-gather.5.cloned.1.call-start = ((), (), s32[]{:S(2)}) async-start(), calls=%async_computation.8 | async-start | bytes 3342336 | tf_op jit(solution)/shard_map/all_gather | solution.py:78
  7.9 105.1 %all-gather.7.cloned.1.call-start = ((), (), s32[]{:S(2)}) async-start(), calls=%async_computation.9 | async-start | bytes 5013504 | tf_op jit(solution)/shard_map/all_gather | solution.py:77
  8.7 158.4 %all-gather.9.cloned.1.call-start = ((), (), s32[]{:S(2)}) async-start(), calls=%async_computation.10 | async-start | bytes 5013504 | tf_op jit(solution)/shard_map/all_gather | solution.py:79
  50.3 62.7 %copy-start.32 = (f32[1536]{0:T(1024)}, f32[1536]{0:T(1024)S(1)}, u32[]{:S(2)}) copy-start(f32[1536]{0:T(1024)S(1)} %convert_element_type.261) | copy-start | bytes 18436
  50.3 120.7 %copy-start.45 = (f32[1536]{0:T(1024)}, f32[1536]{0:T(1024)S(1)}, u32[]{:S(2)}) copy-start(f32[1536]{0:T(1024)S(1)} %convert_element_type.270) | copy-start | bytes 18436
  56.7 18.1 %copy-start.50 = (s32[2048,1]{0,1:T(1,128)}, s32[2048,1]{0,1:T(1,128)S(1)}, u32[]{:S(2)}) copy-start(s32[2048,1]{0,1:T(1,128)S(1)} %compare_select_fusion) | copy-start | bytes 24580
  75.4 42.2 %copy-start.30 = (pred[256,256]{0,1:T(8,128)(4,1)}, pred[256,256]{0,1:T(8,128)(4,1)S(1)}, u32[]{:S(2)}) copy-start(pred[256,256]{0,1:T(8,128)(4,1)S(1)} %iota_compare_fusion) | copy-start | bytes 196612
  75.9 41.5 %copy-start.26 = (f32[256,32]{0,1:T(8,128)}, f32[256,32]{0,1:T(8,128)S(1)}, u32[]{:S(2)}) copy-start(f32[256,32]{0,1:T(8,128)S(1)} %get-tuple-element.43) | copy-start | bytes 98308
  75.9 41.5 %copy-start.28 = (f32[256,32]{0,1:T(8,128)}, f32[256,32]{0,1:T(8,128)S(1)}, u32[]{:S(2)}) copy-start(f32[256,32]{0,1:T(8,128)S(1)} %get-tuple-element.44) | copy-start | bytes 98308
  81.0 39.0 %copy-start.24 = (bf16[256,512]{0,1:T(8,128)(2,1)}, bf16[256,512]{0,1:T(8,128)(2,1)S(1)}, u32[]{:S(2)}) copy-start(bf16[256,512]{0,1:T(8,128)(2,1)S(1)} %copy.84) | copy-start | bytes 786436
  81.1 36.6 %copy-start.34 = (bf16[256,8,32]{0,2,1:T(8,128)(2,1)}, bf16[256,8,32]{0,2,1:T(8,128)(2,1)S(1)}, u32[]{:S(2)}) copy-start(bf16[256,8,32]{0,2,1:T(8,128)(2,1)S(1)} %get-tuple-element.41) | copy-start | bytes 393220
  81.1 36.6 %copy-start.36 = (bf16[256,8,32]{0,2,1:T(8,128)(2,1)}, bf16[256,8,32]{0,2,1:T(8,128)(2,1)S(1)}, u32[]{:S(2)}) copy-start(bf16[256,8,32]{0,2,1:T(8,128)(2,1)S(1)} %get-tuple-element.42) | copy-start | bytes 393220
  122.8 48.2 %copy-start.12 = (bf16[8,64,3,256]{3,1,2,0:T(8,128)(2,1)}, bf16[8,64,3,256]{3,1,2,0:T(8,128)(2,1)S(1)}, u32[]{:S(2)}) copy-start(bf16[8,64,3,256]{3,1,2,0:T(8,128)(2,1)S(1)} %fusion.38) | copy-start | bytes 2359300
  171.0 10.9 copy-start.53
  188.9 178.7 %all-to-all-start = ((bf16[16,160,1536]{2,1,0:T(8,128)(2,1)}), bf16[16,160,1536]{2,1,0:T(8,128)(2,1)}, u32[]{:S(2)}, u32[]{:S(2)}) async-start(bf16[16,160,1536]{2,1,0:T(8,128)(2,1)} %broadcast_select_fusion), calls=%async_computation | async-start | bytes 15728640 | tf_op jit(solution)/shard_map/all_to_all | solution.py:138
  337.3 11.8 copy-start.56
  338.6 11.9 copy-start.44
  338.6 12.2 copy-start.51
  367.6 183.8 %all-to-all-start.2 = ((bf16[16,160,1536]{2,1,0:T(8,128)(2,1)}), bf16[16,160,1536]{2,1,0:T(8,128)(2,1)}, u32[]{:S(2)}, u32[]{:S(2)}) async-start(bf16[16,160,1536]{2,1,0:T(8,128)(2,1)} %multiply_convert_fusion), calls=%async_computation.2 | async-start | bytes 15728640 | tf_op jit(solution)/shard_map/all_to_all | solution.py:178
  570.5 35.6 %copy-start.60 = (bf16[1,1536,512]{2,1,0:T(8,128)(2,1)S(1)}, bf16[1,1536,512]{2,1,0:T(8,128)(2,1)}, u32[]{:S(2)}) copy-start(bf16[1,1536,512]{2,1,0:T(8,128)(2,1)} %param.23) | copy-start | bytes 4718596
  570.5 177.2 %all-to-all-start.1 = ((bf16[16,160,1536]{2,1,0:T(8,128)(2,1)}), bf16[16,160,1536]{2,1,0:T(8,128)(2,1)}, u32[]{:S(2)}, u32[]{:S(2)}) async-start(bf16[16,160,1536]{2,1,0:T(8,128)(2,1)} %bitcast.162), calls=%async_computation.1 | async-start | bytes 15728640 | tf_op jit(solution)/shard_map/all_to_all | solution.py:148
  747.6 34.6 %copy-start.41 = (f32[8,3,256]{2,1,0:T(4,128)S(1)}, f32[8,3,256]{2,1,0:T(4,128)}, u32[]{:S(2)}) copy-start(f32[8,3,256]{2,1,0:T(4,128)} %copy-done.40) | copy-start | bytes 73732
  747.6 34.6 %copy-start.43 = (f32[8,3,256]{2,1,0:T(4,128)S(1)}, f32[8,3,256]{2,1,0:T(4,128)}, u32[]{:S(2)}) copy-start(f32[8,3,256]{2,1,0:T(4,128)} %copy-done.42) | copy-start | bytes 73732
  747.6 176.1 %all-to-all-start.3 = ((bf16[16,160,1536]{2,1,0:T(8,128)(2,1)}), bf16[16,160,1536]{2,1,0:T(8,128)(2,1)}, u32[]{:S(2)}, u32[]{:S(2)}) async-start(bf16[16,160,1536]{2,1,0:T(8,128)(2,1)} %bitcast.161), calls=%async_computation.3 | async-start | bytes 15728640 | tf_op jit(solution)/shard_map/all_to_all | solution.py:192
  782.2 286.5 %reduce-scatter.9.cloned.1.call-start = ((), (), s32[]{:S(2)}) async-start(), calls=%async_computation.12 | async-start | bytes 3342336 | tf_op jit(solution)/shard_map/reduce_scatter | solution.py:251
  972.6 174.3 %reduce-scatter.11.cloned.1.call-start = ((), (), s32[]{:S(2)}) async-start(), calls=%async_computation.13 | async-start | bytes 5013504 | tf_op jit(solution)/shard_map/reduce_scatter | solution.py:254
  977.8 248.0 %reduce-scatter.7.cloned.1.call-start = ((), (), s32[]{:S(2)}) async-start(), calls=%async_computation.11 | async-start | bytes 5013504 | tf_op jit(solution)/shard_map/reduce_scatter | solution.py:248
  985.4 299.1 %reduce-scatter.13.cloned.1.call-start = ((), (), s32[]{:S(2)}) async-start(), calls=%async_computation.14 | async-start | bytes 417792
  1004.9 420.4 %all-reduce.10.cloned.1.call-start = ((), (), s32[]{:S(2)}) async-start(), calls=%async_computation.15 | async-start | bytes 11010048 | tf_op jit(solution)/shard_map/psum | solution.py:264
  1014.8 211.6 %copy-start.16 = (bf16[256,24,64]{0,2,1:T(8,128)(2,1)S(1)}, bf16[256,24,64]{0,2,1:T(8,128)(2,1)}, u32[]{:S(2)}) copy-start(bf16[256,24,64]{0,2,1:T(8,128)(2,1)} %copy-done.15) | copy-start | bytes 2359300
  (49 other events, 218.7 us)
Sparse Core Ops, SparseCore 0:
  10.3 47.9 all-gather.4
  60.6 52.3 all-gather.6
  115.3 51.7 all-gather.8
  972.7 95.8 reduce-scatter.8
  1072.4 74.5 reduce-scatter.10
  1151.1 74.5 reduce-scatter.6
  1229.8 54.6 reduce-scatter.12
  1288.3 136.9 all-reduce.9
where the time goes:
time: 1450 us; the launch traced here: 1440 us
  waiting for transfers between devices  799 us (55%)
  blocking collectives  214 us (15%)
  matrix products  134 us (9%)
  starting transfers between devices  118 us (8%)
  local copies, waits for them, and re-layouts  99 us (7%)
  other arithmetic  62.4 us (4%)
  between operations  17.7 us (1%)
    all_gather x1, blocking collectives, per_device(): lax.all_gather(w_router, 'expert', axis=0, tiled=True)  143 us
    psum x1, waiting for transfers between devices, per_device(): lax.psum(local_shards[2].astype(jnp.bfloat16), 'dp').astype(jnp.float32)  133 us
    all_to_all x1, waiting for transfers between devices, per_device(): lax.all_to_all(grad_out_rows, 'expert', split_axis=0, concat_axis=0, tile...  122 us
    all_to_all x1, waiting for transfers between devices, per_device(): lax.all_to_all(expert_out.reshape(group_size, capacity, model_width), 'ex...  122 us
    all_to_all x1, waiting for transfers between devices, per_device(): lax.all_to_all(d_arrived.reshape(group_size, capacity, model_width), 'exp...  114 us
    reduce_scatter x1, waiting for transfers between devices, per_device(): lax.psum_scatter(grad_query.astype(jnp.bfloat16), 'expert', scatter_dimen...  78.8 us
    reduce_scatter x1, waiting for transfers between devices, per_device(): lax.psum_scatter(grad_out_w.astype(jnp.bfloat16), 'expert', scatter_dimen...  78.3 us
    unnamed x2, blocking collectives  66.7 us
  transfers between devices with their start and end apart: 12, of which 10 were waited for; matrix products, arithmetic and copies ran while one was open for 13% of the time, Pallas kernels for 0%

commit v1 on v0

v1 whole, which is shorter than its diff:
```python
import functools

import jax
import jax.numpy as jnp
from jax import lax
from jax.experimental import pallas as pl
from jax.experimental.pallas import tpu as pltpu
from jax.sharding import PartitionSpec as P

HD = 64
EPSILON = 1e-05
MESH = pl.DeviceIdType.MESH
ANY = pl.BlockSpec(memory_space=pl.ANY)
VMEM = pl.BlockSpec(memory_space=pltpu.VMEM)
DMA = pltpu.SemaphoreType.DMA
MB = 2**20
f32 = jnp.float32
bf16 = jnp.bfloat16


def mul(a, b, ca, cb):
    return lax.dot_general(a, b, (((ca,), (cb,)), ((), ())), preferred_element_type=f32)


class Place:
    def __init__(self, n):
        self.n, self.mid, self.ring = n, n // 8, n // 2
        self.half = self.ring // 2
        self.me = lax.axis_index("expert")
        self.chip, self.core = lax.div(self.me, 2), lax.rem(self.me, 2)
        outer, inner = lax.div(self.chip, self.mid), lax.rem(self.chip, self.mid)
        row = 3 - outer
        step = jnp.where(lax.rem(row, 2) == 0, inner - 1, self.mid - 1 - inner)
        self.at = jnp.where(inner == 0, outer, 4 + row * (self.mid - 1) + step)
        self.sibling = self.chip * 2 + 1 - self.core
        self.right, self.left = self.device(1), self.device(-1)

    def chip_at(self, distance):
        p = lax.rem(self.at + distance + self.ring, self.ring)
        wide = max(self.mid - 1, 1)
        row, k = lax.div(lax.max(p - 4, 0), wide), lax.rem(lax.max(p - 4, 0), wide)
        inner = jnp.where(lax.rem(row, 2) == 0, 1 + k, self.mid - 1 - k)
        return jnp.where(p < 4, p * self.mid, (3 - row) * self.mid + inner)

    def device(self, distance):
        return self.chip_at(distance) * 2 + self.core


def remote(src, dst, send, recv, device):
    return pltpu.make_async_remote_copy(
        src_ref=src, dst_ref=dst, send_sem=send, recv_sem=recv, device_id={"expert": device}, device_id_type=MESH
    )


def meet(targets):
    barrier = pltpu.get_barrier_semaphore()
    for target in targets:
        pl.semaphore_signal(barrier, inc=1, device_id={"expert": target}, device_id_type=MESH)
    pl.semaphore_wait(barrier, len(targets))


def meet_all(place):
    barrier = pltpu.get_barrier_semaphore()

    @pl.loop(1, place.n)
    def _(d):
        other = lax.rem(place.me + d, place.n)
        pl.semaphore_signal(barrier, inc=1, device_id={"expert": other}, device_id_type=MESH)

    pl.semaphore_wait(barrier, place.n - 1)


def column_cuts(width, parts):
    tiles = width // 128
    edges = [128 * (tiles * i // parts) for i in range(parts + 1)]
    return [(edges[i], edges[i + 1] - edges[i]) for i in range(parts)]


def gather_kernel(n, cuts, count, *refs):
    xs, outs, (own_sem, ss, rs, css, crs) = refs[:count], refs[count : 2 * count], refs[2 * count :]
    place = Place(n)
    half = place.half
    meet((place.right, place.left, place.sibling))
    started = []

    def begin(copy):
        copy.start()
        started.append(copy)

    def has(d, k, q, parts):
        return k < half or ((q < parts // 2) == (d == 0))

    for a in range(count):
        x_ref, o_ref = xs[a], outs[a]
        parts = len(cuts[a])
        own = pltpu.make_async_copy(x_ref, o_ref.at[place.me], own_sem.at[a])
        own.start()

        def part(ref, q, a=a):
            return ref.at[:, pl.ds(*cuts[a][q])]

        def along(d, k, q, a=a, x_ref=x_ref, o_ref=o_ref):
            b = place.device(1 - k) if d == 0 else place.device(k - 1)
            src = part(x_ref, q) if k == 1 else part(o_ref.at[b], q)
            return remote(
                src,
                part(o_ref.at[b], q),
                ss.at[a, d, k - 1, q],
                rs.at[a, d, k - 1, q],
                place.right if d == 0 else place.left,
            )

        def across(d, k, q, a=a, x_ref=x_ref, o_ref=o_ref):
            b = place.me if k == 0 else (place.device(-k) if d == 0 else place.device(k))
            src = part(x_ref, q) if k == 0 else part(o_ref.at[b], q)
            return remote(src, part(o_ref.at[b], q), css.at[a, d, k, q], crs.at[a, d, k, q], place.sibling)

        for k in range(1, half + 2):
            for i in range(parts):
                for d in (0, 1):
                    q = i if d == 0 else parts - 1 - i
                    if k > 1 and has(d, k - 1, q, parts):
                        along(d, k - 1, q).wait_recv()
                    if k <= half and has(d, k, q, parts):
                        begin(along(d, k, q))
                    if k == 1 and d == 0:
                        begin(across(0, 0, q))
                    if k > 1 and has(d, k - 1, q, parts):
                        begin(across(d, k - 1, q))
        for k in range(half + 1):
            for q in range(parts):
                for d in (0, 1):
                    if (k == 0 and d == 0) or (k > 0 and has(d, k, q, parts)):
                        across(d, k, q).wait_recv()
        own.wait()
    for copy in started:
        copy.wait_send()


def gather(n, arrays, collective_id):
    half, count = n // 4, len(arrays)
    cuts = [column_cuts(x.shape[1], 2) for x in arrays]
    return pl.pallas_call(
        functools.partial(gather_kernel, n, cuts, count),
        out_shape=[jax.ShapeDtypeStruct((n,) + x.shape, x.dtype) for x in arrays],
        in_specs=[ANY] * count,
        out_specs=[ANY] * count,
        scratch_shapes=[
            DMA((count,)),
            DMA((count, 2, half, 2)),
            DMA((count, 2, half, 2)),
            DMA((count, 2, half + 1, 2)),
            DMA((count, 2, half + 1, 2)),
        ],
        compiler_params=pltpu.CompilerParams(
            collective_id=collective_id, has_side_effects=True, vmem_limit_bytes=16 * MB
        ),
    )(*arrays)


SLOTS = 4


def ring_work(half, parts):
    work = []
    for k in range(half, 0, -1):
        for i in range(parts):
            for d in (0, 1):
                q = i if d == 0 else parts - 1 - i
                if goes(d, k, q, half, parts):
                    work.append((d, k, q))
    return work + [(None, 0, q) for q in range(parts)]


def goes(d, k, q, half, parts):
    return k < half or ((q < parts // 2) == (d == 0))


def widest(width, parts):
    return max(w for _, w in column_cuts(width, parts))


def reduce_scratch(rows, width, half, parts):
    return [
        pltpu.VMEM((2, half, rows, width), bf16),
        pltpu.VMEM((SLOTS, rows, widest(width, parts)), bf16),
        pltpu.VMEM((SLOTS, rows, widest(width, parts)), bf16),
        DMA((SLOTS,)),
        DMA((SLOTS,)),
        DMA((SLOTS,)),
        DMA((2, half, parts)),
    ]


def ring_reduce(place, own_at, other_at, other_wait, width, write, scratch):
    arrived, mine, theirs, mine_sem, theirs_sem, send_sem, recv_sem = scratch
    half = place.half
    parts = recv_sem.shape[2]
    cuts = column_cuts(width, parts)
    rows = arrived.shape[2]
    tile = 16
    work = ring_work(half, parts)

    def chip_of(d, k):
        return place.chip_at(k if d != 1 else -k)

    def loads(i):
        d, k, q = work[i]
        slot, chip, (start, size) = i % SLOTS, chip_of(d, k), cuts[q]
        return (
            pltpu.make_async_copy(
                own_at(chip).at[:, pl.ds(start, size)], mine.at[slot, :, pl.ds(0, size)], mine_sem.at[slot]
            ),
            pltpu.make_async_copy(
                other_at(chip).at[:, pl.ds(start, size)], theirs.at[slot, :, pl.ds(0, size)], theirs_sem.at[slot]
            ),
        )

    def send(i):
        d, k, q = work[i]
        start, size = cuts[q]
        return remote(
            mine.at[i % SLOTS, :, pl.ds(0, size)],
            arrived.at[d, k - 1, :, pl.ds(start, size)],
            send_sem.at[i % SLOTS],
            recv_sem.at[d, k - 1, q],
            place.right if d == 0 else place.left,
        )

    waited = set()

    def fetch(i):
        if i >= len(work):
            return
        d, k, q = work[i]
        if i >= SLOTS:
            send(i - SLOTS).wait_send()
        key = (0 if k in (0, half) else d, k)
        if key not in waited:
            waited.add(key)
            other_wait(chip_of(d, k))
        for copy in loads(i):
            copy.start()

    ahead = SLOTS // 2
    for i in range(ahead):
        fetch(i)
    for i, (d, k, q) in enumerate(work):
        fetch(i + ahead)
        for copy in loads(i):
            copy.wait()
        start, size = cuts[q]
        slot = i % SLOTS
        come = []
        for dd in (0, 1) if d is None else (d,):
            if k + 1 <= half and goes(dd, k + 1, q, half, parts):
                piece = arrived.at[dd, k, :, pl.ds(start, size)]
                remote(piece, piece, send_sem.at[slot], recv_sem.at[dd, k, q], place.sibling).wait_recv()
                come.append(dd)

        @pl.loop(0, rows // tile)
        def _(r):
            at = pl.ds(pl.multiple_of(r * tile, tile), tile)
            total = mine[slot, at, pl.ds(0, size)].astype(f32) + theirs[slot, at, pl.ds(0, size)].astype(f32)
            for dd in come:
                total += arrived[dd, k, at, pl.ds(start, size)].astype(f32)
            if d is None:
                write(at, pl.ds(start, size), total)
            else:
                mine[slot, at, pl.ds(0, size)] = total.astype(bf16)

        if d is not None:
            send(i).start()
        yield
    sends = len(work) - parts
    for i in range(max(0, len(work) - SLOTS), sends):
        send(i).wait_send()


DENSE_PARTS = 4


def swap_halves(values, lane):
    width = values.shape[1]
    return jnp.where(lane % HD < HD // 2, pltpu.roll(values, width - HD // 2, 1), pltpu.roll(values, HD // 2, 1))


def head_halves(block, lane, low):
    turned = pltpu.roll(block, HD, 1)
    lower, upper = (block, turned) if low == 0 else (turned, block)
    zero = jnp.zeros_like(block)
    return jnp.where(lane < HD, lower, zero).astype(bf16), jnp.where(lane < HD, zero, upper).astype(bf16)


def softmax_rows(q, k, causal):
    scores = jnp.where(causal, mul(q, k, 1, 1) * HD**-0.5, -1e30)
    e = jnp.exp(scores - jnp.max(scores, axis=1, keepdims=True))
    return e * (1.0 / jnp.sum(e, axis=1, keepdims=True))


def backward_kernel(
    n,
    dp,
    od_ref,
    sd_ref,
    wall_ref,
    dmix_ref,
    dgate_ref,
    gates_ref,
    middle_ref,
    mixed_ref,
    dout_ref,
    tokens_ref,
    normed_t_ref,
    attended_t_ref,
    q_ref,
    k_ref,
    v_ref,
    cos_ref,
    sin_ref,
    gains_ref,
    output_ref,
    input_grad_ref,
    dense_ref,
    weights,
    extra_w,
    d_middle,
    d_middle_low,
    d_att,
    d_qkv,
    d_normed,
    extra,
    logits_low,
    own_f,
    stage_f,
    other_f,
    come_f,
    copies_f,
    weight_sem,
    stage_sem,
    other_sem,
    send_f,
    recv_f,
    copy_s,
    copy_r,
    *scratch_d,
):
    place = Place(n)
    half, ring = place.half, place.ring
    rank = lax.axis_index("dp")
    rows, width = middle_ref.shape
    q_width, kv_width = q_ref.shape[1], 2 * k_ref.shape[1]
    qkv_width = q_width + kv_width
    shard = own_f.shape[1]
    full_width = own_f.shape[2]
    barrier = pltpu.get_barrier_semaphore()
    for target in (place.right, place.left, place.sibling):
        pl.semaphore_signal(barrier, inc=1, device_id={"expert": target}, device_id_type=MESH)
    for turn in range(1, dp):
        pl.semaphore_signal(barrier, inc=1, device_id={"dp": lax.rem(rank + turn, dp)}, device_id_type=MESH)
    out_w = pltpu.make_async_copy(
        wall_ref.at[:, pl.ds(qkv_width, width)], weights.at[:, pl.ds(0, width)], weight_sem.at[0]
    )
    extra_copy = pltpu.make_async_copy(wall_ref.at[:, pl.ds(qkv_width + width, 128)], extra_w, weight_sem.at[1])
    qkv_w = pltpu.make_async_copy(wall_ref.at[:, pl.ds(0, qkv_width)], weights, weight_sem.at[2])
    out_w.start()
    extra_copy.start()
    pl.semaphore_wait(barrier, 3 + dp - 1)

    def write_output(at, columns, total):
        output_ref[at, columns] = (middle_ref[at, columns] + total).astype(bf16)

    background = ring_reduce(
        place, lambda chip: od_ref.at[chip], lambda chip: sd_ref.at[chip], lambda chip: None, width, write_output, scratch_d
    )
    items = len(ring_work(half, scratch_d[6].shape[2]))
    done = [0]

    def pump(share):
        while done[0] < min(items, int(items * share + 0.5)):
            next(background)
            done[0] += 1

    pump(0.07)
    d_rows = jnp.concatenate([dgate_ref[:, 0, :], jnp.zeros((128 - n, rows), f32)], axis=0)
    d_gates = jnp.transpose(d_rows)
    gates = gates_ref[...]
    d_sel = gates * (d_gates - jnp.sum(gates * d_gates, axis=1, keepdims=True))
    logits_low[...] = d_sel.astype(bf16)
    extra_copy.wait()
    d_normed[...] = mul(logits_low[...], extra_w[...], 1, 1)
    gain_one, gain_two = gains_ref[0:1], gains_ref[1:2]
    tile = 32

    @pl.loop(0, rows // tile)
    def _(r):
        at = pl.ds(pl.multiple_of(r * tile, tile), tile)
        middle = middle_ref[at]
        d_mixed = dmix_ref[at] + d_normed[at]
        inv = lax.rsqrt(jnp.mean(middle * middle, axis=1, keepdims=True) + EPSILON)
        scaled = d_mixed * gain_two
        back = jnp.mean(scaled * middle, axis=1, keepdims=True)
        total = dout_ref[at].astype(f32) + inv * scaled - middle * (inv * inv * inv * back)
        d_middle[at] = total
        d_middle_low[at] = total.astype(bf16)
        d_att[at] = (d_mixed * middle * inv).astype(bf16)

    lane = lax.broadcasted_iota(jnp.int32, (rows, 128), 1)
    extra[...] = mul(mixed_ref[...], logits_low[...], 0, 0) + mul(
        d_att[...], (lane == n + 1).astype(bf16), 0, 0
    )
    pump(0.14)
    out_w.wait()
    d_att[...] = mul(d_middle_low[...], weights[:, pl.ds(0, width)], 1, 1).astype(bf16)
    qkv_w.start()
    pump(0.21)

    t_at = lax.broadcasted_iota(jnp.int32, (rows, rows), 0)
    u_at = lax.broadcasted_iota(jnp.int32, (rows, rows), 1)
    causal = t_at >= u_at
    cosine, sine = cos_ref[...], sin_ref[...]
    sine_back = jnp.where(lane % HD < HD // 2, sine, -sine)
    kv_count = k_ref.shape[1] // HD
    per_group = q_width // HD // kv_count
    d_normed[...] = jnp.zeros_like(d_normed)
    pair_k, pair_v = None, None
    for g in range(kv_count):
        pair = pl.ds(128 * (g // 2), 128)
        k_parts = head_halves(k_ref[:, pair].astype(f32), lane, g % 2)
        v_parts = head_halves(v_ref[:, pair].astype(f32), lane, g % 2)
        d_k, d_v = [None, None], [None, None]
        for h in range(per_group * g, per_group * (g + 1)):
            at = pl.ds(128 * (h // 2), 128)
            low = h % 2
            query, d_a = q_ref[:, at], d_att[:, at]
            probs = softmax_rows(query, k_parts[low], causal)
            probs_low = probs.astype(bf16)
            d_probs = mul(d_a, v_parts[low], 1, 1)
            weighted = probs * d_probs
            d_scores = (weighted - probs * jnp.sum(weighted, axis=1, keepdims=True)).astype(bf16)
            d_normed[:, at] += mul(d_scores, k_parts[low], 1, 0)
            step_k, step_v = mul(d_scores, query, 0, 0), mul(probs_low, d_a, 0, 0)
            d_k[low] = step_k if d_k[low] is None else d_k[low] + step_k
            d_v[low] = step_v if d_v[low] is None else d_v[low] + step_v

        def gathered(parts):
            stay, turn = parts[g % 2], parts[1 - g % 2]
            return stay if turn is None else (pltpu.roll(turn, HD, 1) if stay is None else stay + pltpu.roll(turn, HD, 1))

        if g % 2 == 0:
            pair_k, pair_v = gathered(d_k), gathered(d_v)
        if g % 2 == 1 or g + 1 == kv_count:
            total_k = jnp.where(lane < HD, pair_k, gathered(d_k)) * HD**-0.5
            total_v = jnp.where(lane < HD, pair_v, gathered(d_v))
            turned = total_k * cosine + swap_halves(total_k, lane) * sine_back
            d_qkv[:, pl.ds(q_width + 128 * (g // 2), 128)] = turned.astype(bf16)
            d_qkv[:, pl.ds(q_width + kv_width // 2 + 128 * (g // 2), 128)] = total_v.astype(bf16)
        pump(0.21 + 0.6 * (g + 1) / kv_count)
    for b in range(q_width // 128):
        at = pl.ds(128 * b, 128)
        total = d_normed[:, at] * HD**-0.5
        d_qkv[:, at] = (total * cosine + swap_halves(total, lane) * sine_back).astype(bf16)
    pump(0.85)
    qkv_w.wait()
    d_normed[...] = mul(d_qkv[...], weights[...], 1, 1)

    @pl.loop(0, rows // tile)
    def _(r):
        at = pl.ds(pl.multiple_of(r * tile, tile), tile)
        inputs = tokens_ref[at].astype(f32)
        d = d_normed[at]
        inv = lax.rsqrt(jnp.mean(inputs * inputs, axis=1, keepdims=True) + EPSILON)
        scaled = d * gain_one
        back = jnp.mean(scaled * inputs, axis=1, keepdims=True)
        total = d_middle[at] + inv * scaled - inputs * (inv * inv * inv * back)
        input_grad_ref[at] = total.astype(bf16)
        d_att[at] = (d * inputs * inv).astype(bf16)

    extra[...] += mul(d_att[...], (lane == n).astype(bf16), 0, 0)
    pump(1.0)
    for _ in background:
        pass

    def cross(chip, slot):
        return remote(stage_f.at[slot], other_f.at[chip], stage_sem.at[slot], other_sem.at[chip], place.sibling)

    def fill(ref, device):
        at = pl.ds(pl.multiple_of(device * shard, 16), shard)
        ref[:, pl.ds(0, qkv_width)] = mul(normed_t_ref[at], d_qkv[...], 1, 0).astype(bf16)
        ref[:, pl.ds(qkv_width, width)] = mul(attended_t_ref[at], d_middle_low[...], 1, 0).astype(bf16)
        ref[:, pl.ds(qkv_width + width, 128)] = extra[at].astype(bf16)

    @pl.loop(0, ring)
    def _(i):
        away = half - lax.div(i + 1, 2)
        chip = place.chip_at(jnp.where(lax.rem(i, 2) == 0, away, -away))
        slot = lax.rem(i, 2)

        @pl.when(i >= 2)
        def _():
            cross(chip, slot).wait_send()

        fill(stage_f.at[slot], chip * 2 + 1 - place.core)
        cross(chip, slot).start()
        fill(own_f.at[chip], chip * 2 + place.core)

    for slot in range(2):
        cross(place.chip, slot).wait_send()
    cuts = column_cuts(full_width, DENSE_PARTS)
    work = ring_work(half, DENSE_PARTS)

    def send(d, k, q):
        chip = place.chip_at(k if d == 0 else -k)
        at = pl.ds(*cuts[q])
        return remote(
            own_f.at[chip, :, at],
            come_f.at[d, k - 1, :, at],
            send_f.at[d, k - 1, q],
            recv_f.at[d, k - 1, q],
            place.right if d == 0 else place.left,
        )

    def spread(turn, q):
        at = pl.ds(*cuts[q])
        return pltpu.make_async_remote_copy(
            src_ref=copies_f.at[rank, :, at],
            dst_ref=copies_f.at[rank, :, at],
            send_sem=copy_s.at[turn, q],
            recv_sem=copy_r.at[turn, q],
            device_id={"dp": lax.rem(rank + turn, dp)},
            device_id_type=MESH,
        )

    met = set()
    for d, k, q in work:
        chip = place.chip_at(0 if d is None else (k if d == 0 else -k))
        key = (0 if k in (0, half) else d, k)
        if key not in met:
            met.add(key)
            remote(other_f.at[chip], other_f.at[chip], stage_sem.at[0], other_sem.at[chip], place.sibling).wait_recv()
        at = pl.ds(*cuts[q])
        total = own_f[chip, :, at].astype(f32) + other_f[chip, :, at].astype(f32)
        for dd in (0, 1) if d is None else (d,):
            if k + 1 <= half and goes(dd, k + 1, q, half, DENSE_PARTS):
                piece = come_f.at[dd, k, :, at]
                remote(piece, piece, send_f.at[dd, k, q], recv_f.at[dd, k, q], place.sibling).wait_recv()
                total += piece[...].astype(f32)
        if d is not None:
            own_f[chip, :, at] = total.astype(bf16)
            send(d, k, q).start()
        else:
            copies_f[rank, :, at] = total.astype(bf16)
            for turn in range(1, dp):
                spread(turn, q).start()
    for q in range(DENSE_PARTS):
        for turn in range(1, dp):
            spread(turn, q).wait()
        at = pl.ds(*cuts[q])
        total = copies_f[0, :, at].astype(f32)
        for r in range(1, dp):
            total += copies_f[r, :, at].astype(f32)
        dense_ref[:, at] = total
    for d, k, q in work:
        if d is not None:
            send(d, k, q).wait_send()


def backward(n, dp, own_d, other_d, wall, others, collective_id):
    half, ring = n // 4, n // 2
    rows, width = own_d.shape[1:]
    full_width = wall.shape[1]
    qkv_width = full_width - width - 128
    shard = wall.shape[0] // n
    q_width = others[9].shape[1]
    return pl.pallas_call(
        functools.partial(backward_kernel, n, dp),
        out_shape=[
            jax.ShapeDtypeStruct((rows, width), bf16),
            jax.ShapeDtypeStruct((rows, width), bf16),
            jax.ShapeDtypeStruct((shard, full_width), f32),
        ],
        in_specs=[ANY] * 3 + [VMEM] * len(others),
        out_specs=[VMEM] * 3,
        scratch_shapes=[
            pltpu.VMEM((width, qkv_width), bf16),
            pltpu.VMEM((width, 128), bf16),
            pltpu.VMEM((rows, width), f32),
            pltpu.VMEM((rows, width), bf16),
            pltpu.VMEM((rows, q_width), bf16),
            pltpu.VMEM((rows, qkv_width), bf16),
            pltpu.VMEM((rows, width), f32),
            pltpu.VMEM((width, 128), f32),
            pltpu.VMEM((rows, 128), bf16),
            pltpu.VMEM((ring, shard, full_width), bf16),
            pltpu.VMEM((2, shard, full_width), bf16),
            pltpu.VMEM((ring, shard, full_width), bf16),
            pltpu.VMEM((2, half, shard, full_width), bf16),
            pltpu.VMEM((dp, shard, full_width), bf16),
            DMA((3,)),
            DMA((2,)),
            DMA((ring,)),
            DMA((2, half, DENSE_PARTS)),
            DMA((2, half, DENSE_PARTS)),
            DMA((dp, DENSE_PARTS)),
            DMA((dp, DENSE_PARTS)),
        ]
        + reduce_scratch(rows, width, half, 4),
        compiler_params=pltpu.CompilerParams(
            collective_id=collective_id, has_side_effects=True, vmem_limit_bytes=63 * MB
        ),
    )(own_d, other_d, wall, *others)


QUARTERS = 4


def expert_kernel(
    n,
    x_ref,
    dog_ref,
    gates_ref,
    wgu_ref,
    wd_ref,
    de_ref,
    dgates_ref,
    ggu_ref,
    gd_ref,
    od_ref,
    sd_ref,
    oe_ref,
    se_ref,
    xg_ref,
    acc_gu,
    acc_d,
    gate_in,
    dgate_out,
    xbuf,
    dobuf,
    pd,
    pe,
    own_sem,
    ring_s,
    ring_r,
    cross_s,
    cross_r,
    load_sem,
    put_sem,
    sib_r,
    gate_s,
    gate_r,
    dgate_s,
    dgate_r,
    *reduce_refs,
):
    place = Place(n)
    half, ring, me = place.half, place.ring, place.me
    rows, width = x_ref.shape
    hidden_width = wd_ref.shape[0]
    piece = rows // QUARTERS
    meet_all(place)

    own = pltpu.make_async_copy(x_ref, xg_ref.at[me], own_sem.at[0])
    own.start()

    def at(q):
        return pl.ds(pl.multiple_of(q * piece, piece), piece)

    def block_of(d, k):
        return jnp.where(d == 0, place.device(-k), place.device(k))

    def along(d, k, q):
        b = block_of(d, k - 1)
        return remote(
            xg_ref.at[b, at(q)],
            xg_ref.at[b, at(q)],
            ring_s.at[d, k - 1, q],
            ring_r.at[d, k - 1, q],
            jnp.where(d == 0, place.right, place.left),
        )

    def across(d, k, q):
        b = block_of(d, k)
        return remote(xg_ref.at[b, at(q)], xg_ref.at[b, at(q)], cross_s.at[d, k, q], cross_r.at[d, k, q], place.sibling)

    def gate_copy(d):
        to = lax.rem(me + d, n)
        return remote(gates_ref.at[to], gate_in.at[me], gate_s.at[d], gate_r.at[d], to)

    @pl.loop(1, n)
    def _(d):
        gate_copy(d).start()

    own.wait()
    for q in range(QUARTERS):
        for d in (0, 1):
            along(d, 1, q).start()
    for q in range(QUARTERS):
        across(0, 0, q).start()
    gate_in[me] = gates_ref[me]
    acc_gu[...] = jnp.zeros_like(acc_gu)
    acc_d[...] = jnp.zeros_like(acc_d)

    def step_of(i):
        k = jnp.where(i < 2, 0, lax.div(i + 2, 4))
        j = jnp.where(i < 2, i, lax.rem(i + 2, 4))
        edge = jnp.logical_or(k == 0, k == half)
        d = jnp.where(edge, 0, lax.rem(j, 2))
        other = jnp.where(edge, j, lax.div(j, 2))
        chip = jnp.where(d == 0, place.chip_at(-k), place.chip_at(k))
        core = jnp.where(other == 0, place.core, 1 - place.core)
        return k, j, d, other, chip, chip * 2 + core

    def pump(d, k, q, last=False):
        along(d, k, q).wait_recv()
        if not last:
            near = jnp.where(q < QUARTERS // 2, 0, 1) == d

            @pl.when(jnp.logical_or(k + 1 < half, near))
            def _():
                along(d, k + 1, q).start()

        across(d, k, q).start()

    def load(block, slot):
        return (
            pltpu.make_async_copy(xg_ref.at[block], xbuf.at[slot], load_sem.at[0, slot]),
            pltpu.make_async_copy(dog_ref.at[block], dobuf.at[slot], load_sem.at[1, slot]),
        )

    def put_wait(slot):
        for which, buf in enumerate((pd, pe)):
            pltpu.make_async_copy(buf.at[slot], buf.at[slot], put_sem.at[which, slot]).wait()

    def dgate_copy(block):
        d = lax.rem(block - me + n, n)
        return remote(dgate_out.at[block], dgates_ref.at[me], dgate_s.at[d], dgate_r.at[d], block)

    for copy in load(me, 0):
        copy.start()

    @pl.loop(0, n)
    def _(i):
        k, j, d, other, chip, block = step_of(i)
        slot = lax.rem(i, 2)
        for copy in load(block, slot):
            copy.wait()

        @pl.when(i > 0)
        def _():
            away = lax.rem(me - block + n, n)
            remote(gate_in.at[block], gate_in.at[block], gate_s.at[away], gate_r.at[away], place.sibling).wait_recv()

        gate = jnp.transpose(gate_in[block])[:, :1]
        x = xbuf[slot]
        gu = mul(x, wgu_ref[...], 1, 0)
        g, u = gu[:, :hidden_width], gu[:, hidden_width:]
        s = 1.0 / (1.0 + jnp.exp(-g))
        gs = g * s
        hid = gs * u
        hidg = (hid * gate).astype(bf16)

        @pl.when(i >= 2)
        def _():
            put_wait(slot)

        pd[slot] = mul(hidg, wd_ref[...], 1, 0).astype(bf16)

        @pl.when(i < 2)
        def _():
            for t in range(2):
                for dd in (0, 1):
                    pump(dd, 1, i * 2 + t)

        @pl.when(jnp.logical_and(i >= 2, k + 1 < half))
        def _():
            for dd in (0, 1):
                pump(dd, k + 1, j)

        @pl.when(k + 1 == half)
        def _():
            pump(jnp.where(j < QUARTERS // 2, 0, 1), half, j, last=True)

        nk, nj, nd, nother, nchip, nblock = step_of(i + 1)

        @pl.when(jnp.logical_and(i + 1 < n, nother == 1))
        def _():
            for q in range(QUARTERS):
                dd = jnp.where(nk == half, 0 if q < QUARTERS // 2 else 1, nd)
                b = nblock
                remote(
                    xg_ref.at[b, at(q)], xg_ref.at[b, at(q)], cross_s.at[dd, nk, q], cross_r.at[dd, nk, q], place.sibling
                ).wait_recv()

        @pl.when(i + 1 < n)
        def _():
            for copy in load(nblock, 1 - slot):
                copy.start()

        do = dobuf[slot]
        dh = mul(do, wd_ref[...], 1, 1)
        dgate = jnp.sum(dh * hid, axis=1, keepdims=True)
        dgate_out[block] = jnp.transpose(jnp.broadcast_to(dgate, (rows, 128)))[:8]
        dh = dh * gate
        d_g = (dh * u * s * (1.0 + g * (1.0 - s))).astype(bf16)
        d_u = (dh * gs).astype(bf16)
        dgu = jnp.concatenate([d_g, d_u], axis=1)
        pe[slot] = mul(dgu, wgu_ref[...], 1, 1).astype(bf16)

        @pl.when(i > 0)
        def _():
            dgate_copy(block).start()

        @pl.when(i == 0)
        def _():
            dgates_ref[me] = dgate_out[me]

        @pl.when(other == 0)
        def _():
            pltpu.make_async_copy(pd.at[slot], od_ref.at[chip], put_sem.at[0, slot]).start()
            pltpu.make_async_copy(pe.at[slot], oe_ref.at[chip], put_sem.at[1, slot]).start()

        @pl.when(other == 1)
        def _():
            remote(pd.at[slot], sd_ref.at[chip], put_sem.at[0, slot], sib_r.at[0, chip], place.sibling).start()
            remote(pe.at[slot], se_ref.at[chip], put_sem.at[1, slot], sib_r.at[1, chip], place.sibling).start()

        acc_gu[...] += mul(x, dgu, 0, 0)
        acc_d[...] += mul(hidg, do, 0, 0)

    put_wait(0)
    put_wait(1)
    ggu_ref[...] = acc_gu[...].astype(bf16)
    gd_ref[...] = acc_d[...].astype(bf16)

    def other_wait(chip):
        remote(se_ref.at[chip], se_ref.at[chip], put_sem.at[1, 0], sib_r.at[1, chip], place.sibling).wait_recv()

    def write(at, columns, total):
        de_ref[at, columns] = total

    for _ in ring_reduce(
        place, lambda chip: oe_ref.at[chip], lambda chip: se_ref.at[chip], other_wait, width, write, reduce_refs
    ):
        pass

    @pl.loop(0, ring)
    def _(chip):
        remote(sd_ref.at[chip], sd_ref.at[chip], put_sem.at[0, 0], sib_r.at[0, chip], place.sibling).wait_recv()

    @pl.loop(1, n)
    def _(d):
        gate_copy(d).wait_send()
        source = lax.rem(me - d + n, n)
        remote(dgates_ref.at[source], dgates_ref.at[source], dgate_s.at[d], dgate_r.at[d], place.sibling).wait()

    for q in range(QUARTERS):
        across(0, 0, q).wait_send()
        for d in (0, 1):
            for k in range(1, half + 1):
                if k < half or ((q < QUARTERS // 2) == (d == 0)):
                    along(d, k, q).wait_send()
                    across(d, k, q).wait_send()


def experts(n, mixed_in, d_gathered, gate_rows, wgu, wd, collective_id):
    half, ring = n // 4, n // 2
    rows, width = mixed_in.shape
    blocks = jax.ShapeDtypeStruct((ring, rows, width), bf16)
    hidden_width = wd.shape[0]
    out = pl.pallas_call(
        functools.partial(expert_kernel, n),
        out_shape=[
            jax.ShapeDtypeStruct((rows, width), f32),
            jax.ShapeDtypeStruct((n, 8, rows), f32),
            jax.ShapeDtypeStruct(wgu.shape, bf16),
            jax.ShapeDtypeStruct(wd.shape, bf16),
            blocks,
            blocks,
            blocks,
            blocks,
            jax.ShapeDtypeStruct((n, rows, width), bf16),
        ],
        in_specs=[ANY, ANY, VMEM, VMEM, VMEM],
        out_specs=[VMEM, VMEM, VMEM, VMEM, ANY, ANY, ANY, ANY, ANY],
        scratch_shapes=[
            pltpu.VMEM(wgu.shape, f32),
            pltpu.VMEM(wd.shape, f32),
            pltpu.VMEM((n, 8, rows), f32),
            pltpu.VMEM((n, 8, rows), f32),
            pltpu.VMEM((2, rows, width), bf16),
            pltpu.VMEM((2, rows, width), bf16),
            pltpu.VMEM((2, rows, width), bf16),
            pltpu.VMEM((2, rows, width), bf16),
            DMA((1,)),
            DMA((2, half, QUARTERS)),
            DMA((2, half, QUARTERS)),
            DMA((2, half + 1, QUARTERS)),
            DMA((2, half + 1, QUARTERS)),
            DMA((2, 2)),
            DMA((2, 2)),
            DMA((2, ring)),
            DMA((n,)),
            DMA((n,)),
            DMA((n,)),
            DMA((n,)),
        ]
        + reduce_scratch(rows, width, half, 2),
        compiler_params=pltpu.CompilerParams(
            collective_id=collective_id, has_side_effects=True, vmem_limit_bytes=62 * MB
        ),
    )(mixed_in, d_gathered, gate_rows, wgu, wd)
    return out[:6]


def rotate(values, cosine, sines):
    half_dim = values.shape[-1] // 2
    first_half = values[..., :half_dim]
    second_half = values[..., half_dim:]
    return jnp.concatenate(
        [first_half * cosine - second_half * sines, second_half * cosine + first_half * sines], -1
    )


def rope_tables(length, head_dim):
    half_dim = head_dim // 2
    positions = jnp.arange(length).astype(f32)
    inverse = jnp.power(f32(10000.0), -jnp.arange(half_dim).astype(f32) / half_dim)
    angles = positions[:, None] * inverse[None, :]
    return (jnp.cos(angles)[:, None, :], jnp.sin(angles)[:, None, :])


def dp_sum(value, size):
    if size == 2:
        return value.astype(f32) + lax.ppermute(value, "dp", [(0, 1), (1, 0)]).astype(f32)
    return lax.psum(value, "dp").astype(f32)


def per_device(
    n,
    dp,
    tokens,
    cotangent,
    lengths,
    routes,
    norm1_gain,
    w_query,
    w_kv,
    w_out,
    norm2_gain,
    w_router,
    expert_gate,
    expert_up,
    expert_down,
):
    tok_rows, model_width = tokens.shape
    expert_count = w_router.shape[1]
    head_dim = HD
    kv_width, q_width = w_kv.shape[1], w_query.shape[1]
    kv_count = kv_width // (2 * head_dim)
    head_count = q_width // head_dim
    per_group = head_count // kv_count
    score_scale = head_dim ** (-0.5)
    shard = w_query.shape[0]
    live = (jnp.arange(tok_rows) < lengths[0]).astype(f32)
    d_out_low = (cotangent.astype(f32) * live[:, None]).astype(bf16)
    extra = jnp.concatenate(
        [
            w_router,
            norm1_gain[:, None],
            norm2_gain[:, None],
            jnp.zeros((shard, 128 - expert_count - 2), bf16),
        ],
        axis=1,
    )
    wall, d_gathered = gather(n, [jnp.concatenate([w_query, w_kv, w_out, extra], axis=1), d_out_low], 0)
    wall = wall.reshape(-1, wall.shape[-1])
    edges = [0, q_width, q_width + kv_width, q_width + kv_width + model_width]
    query_w, kv_w, out_w = (wall[:, a:b] for a, b in zip(edges[:-1], edges[1:]))
    router_w = wall[:, edges[3] : edges[3] + expert_count]
    gain_one = wall[:, edges[3] + expert_count].astype(f32)
    gain_two = wall[:, edges[3] + expert_count + 1].astype(f32)

    inputs = tokens.astype(f32)
    inv_one = lax.rsqrt(jnp.mean(inputs * inputs, axis=-1, keepdims=True) + EPSILON)
    normed_one = (inputs * inv_one * gain_one).astype(bf16)
    query_proj = jnp.dot(normed_one, query_w, preferred_element_type=f32)
    kv_proj = jnp.dot(normed_one, kv_w, preferred_element_type=f32)
    cosine, sines = rope_tables(tok_rows, head_dim)
    queries = (
        rotate(query_proj.reshape(tok_rows, head_count, head_dim), cosine, sines)
        .astype(bf16)
        .reshape(tok_rows, kv_count, per_group, head_dim)
    )
    keys = rotate(
        kv_proj[:, : kv_count * head_dim].reshape(tok_rows, kv_count, head_dim), cosine, sines
    ).astype(bf16)
    values = kv_proj[:, kv_count * head_dim :].reshape(tok_rows, kv_count, head_dim).astype(bf16)
    causal = jnp.arange(tok_rows)[:, None] >= jnp.arange(tok_rows)[None, :]

    def masked_scores():
        scores = (
            jnp.einsum("tgjd,ugd->gjtu", queries, keys, preferred_element_type=f32) * score_scale
        )
        return jnp.where(causal[None, None], scores, -1e30)

    masked = masked_scores()
    row_peak = jnp.max(masked, axis=-1, keepdims=True)
    exp_scores = jnp.exp(masked - row_peak)
    row_total = jnp.sum(exp_scores, axis=-1, keepdims=True)
    probs_low = (exp_scores / row_total).astype(bf16)
    attended = (
        jnp.einsum("gjtu,ugd->tgjd", probs_low, values, preferred_element_type=f32)
        .astype(bf16)
        .reshape(tok_rows, head_count * head_dim)
    )
    middle = inputs + jnp.dot(attended, out_w, preferred_element_type=f32)
    inv_two = lax.rsqrt(jnp.mean(middle * middle, axis=-1, keepdims=True) + EPSILON)
    mixed_in = (middle * inv_two * gain_two).astype(bf16)
    logits = jnp.dot(mixed_in, router_w, preferred_element_type=f32)
    chosen = jnp.any(routes[:, :, None] == jnp.arange(expert_count)[None, None, :], axis=1)
    chosen_logits = jnp.where(chosen, logits, -jnp.inf)
    weights = jnp.exp(chosen_logits - jnp.max(chosen_logits, axis=-1, keepdims=True))
    gates = weights / jnp.sum(weights, axis=-1, keepdims=True)

    gate_rows = jnp.broadcast_to(gates.T[:, None, :], (expert_count, 8, tok_rows))
    wgu = jnp.concatenate([expert_gate[0], expert_up[0]], axis=1)
    d_mixed_experts, d_gate_rows, grad_gu, grad_down, own_d, other_d = experts(
        n, mixed_in, d_gathered, gate_rows, wgu, expert_down[0], 1
    )

    turns = [jnp.tile(table.reshape(tok_rows, -1), (1, 4)) for table in (cosine, sines)]
    gains = jnp.concatenate([gain_one[None], gain_two[None], jnp.zeros((6, model_width), f32)])
    output, input_grad, dense_sum = backward(
        n,
        dp,
        own_d,
        other_d,
        wall,
        (
            d_mixed_experts,
            d_gate_rows,
            jnp.pad(gates, ((0, 0), (0, 128 - expert_count))),
            middle,
            mixed_in,
            d_out_low,
            tokens,
            normed_one.T,
            attended.T,
            queries.reshape(tok_rows, -1),
            keys.reshape(tok_rows, -1),
            values.reshape(tok_rows, -1),
            *turns,
            gains,
        ),
        2,
    )
    grad_gu = dp_sum(grad_gu, dp)
    grad_down = dp_sum(grad_down, dp)
    hidden_width = grad_gu.shape[1] // 2
    return (
        output,
        input_grad,
        dense_sum[:, edges[3] + expert_count],
        dense_sum[:, : edges[1]],
        dense_sum[:, edges[1] : edges[2]],
        dense_sum[:, edges[2] : edges[3]],
        dense_sum[:, edges[3] + expert_count + 1],
        dense_sum[:, edges[3] : edges[3] + expert_count],
        grad_gu[None, :, :hidden_width],
        grad_gu[None, :, hidden_width:],
        grad_down[None],
    )


def solution(mesh):
    rows, own = P(("dp", "expert"), None), P("expert", None)
    expert = P("expert", None, None)
    return jax.shard_map(
        functools.partial(per_device, mesh.shape["expert"], mesh.shape["dp"]),
        mesh=mesh,
        in_specs=(rows, rows, P(("dp", "expert")), rows, P("expert"), own, own, own, P("expert"), own)
        + (expert,) * 3,
        out_specs=(rows, rows, P("expert"), own, own, own, P("expert"), own) + (expert,) * 3,
        check_vma=False,
    )
```

time: 1450 us -> 567 us (0.39)
  waiting for transfers between devices: 799 us -> 0.01 us
  Pallas kernels: 0 us -> 482 us
  blocking collectives: 214 us -> 0 us
  matrix products: 134 us -> 16.7 us
  starting transfers between devices: 118 us -> 2.09 us
  local copies, waits for them, and re-layouts: 99 us -> 36.4 us
  other arithmetic: 62.4 us -> 20.4 us
  between operations: 17.7 us -> 2.1 us
    pallas_call x0 -> x3, Pallas kernels: none -> 482 us  [the longest x1 192 us: experts(): pl.pallas_call(functools.partial(expert_kernel, n), out_shape=[jax.ShapeD...]
    all_to_all x4 -> x0, waiting for transfers between devices: 358 us -> none  [the longest x1 122 us: per_device(): lax.all_to_all(grad_out_rows, 'expert', split_axis=0, concat_axis=0, tile...]
    reduce_scatter x3 -> x0, waiting for transfers between devices: 211 us -> none  [the longest x1 78.8 us: per_device(): lax.psum_scatter(grad_query.astype(jnp.bfloat16), 'expert', scatter_dimen...]
    all_gather x1 -> x0, blocking collectives: 143 us -> none  [per_device(): lax.all_gather(w_router, 'expert', axis=0, tiled=True)]
    psum x1 -> x0, waiting for transfers between devices: 133 us -> none  [per_device(): lax.psum(local_shards[2].astype(jnp.bfloat16), 'dp').astype(jnp.float32)]
    dot_general x21 -> x0, matrix products: 119 us -> none  [the longest x1 12.7 us: per_device(): d_hidden = jnp.dot(grad_arrived, down_mat.T, preferred_element_type=f32)]
    all_to_all x4 -> x0, starting transfers between devices: 117 us -> none  [the longest x1 42.2 us: per_device(): lax.all_to_all(grad_out_rows, 'expert', split_axis=0, concat_axis=0, tile...]
    all_gather x3 -> x0, waiting for transfers between devices: 76.3 us -> none  [the longest x1 44.4 us: per_device(): lax.all_gather(w_out, 'expert', axis=0, tiled=True)]
  transfers between devices with their start and end apart: 12 -> 2, of which waited for: 10 -> 0; matrix products, arithmetic and copies ran while one was open for 13% -> 3% of each run, Pallas kernels for 0% -> 28%
where the time goes in v1:
time: 567 us; the launch traced here: 560 us
  Pallas kernels  482 us (85%)
  local copies, waits for them, and re-layouts  36.4 us (6%)
  other arithmetic  20.4 us (4%)
  matrix products  16.7 us (3%)
    pallas_call x1, Pallas kernels, experts(): pl.pallas_call(functools.partial(expert_kernel, n), out_shape=[jax.ShapeD...  192 us
    pallas_call x1, Pallas kernels, backward(): pl.pallas_call(functools.partial(backward_kernel, n, dp), out_shape=[jax....  159 us
    pallas_call x1, Pallas kernels, gather(): pl.pallas_call(functools.partial(gather_kernel, n, cuts, count), out_shap...  132 us
    unnamed x65, local copies, waits for them, and re-layouts  13.8 us
  transfers between devices with their start and end apart: 2, of which 0 were waited for; matrix products, arithmetic and copies ran while one was open for 3% of the time, Pallas kernels for 28%

profile of v1, /device:TPU:0, one launch (start us, length us, event | category | flops | bytes accessed | tf_op | source)
XLA Modules:
  0.0 560.0 jit_solution(5807014212543345459)
XLA Ops:
  1.4 0.8 copy.68
  3.8 1.3 multiply_convert_fusion.1.refs_1_.dout_ref
  5.1 1.6 concatenate.24.refs_0_
  6.7 131.6 %shard_map.212 = (bf16[16,96,4224]{2,1,0:T(8,128)(2,1)S(1)}, bf16[16,256,1536]{2,1,0:T(8,128)(2,1)S(1)}) custom-call(bf16[96,4224]{1,0:T(8,128)(2,1)S(1)} %concatenate.24.refs_0_, bf16[256,1536]{1,0:T(8,128)(2,1)S(1)} %multiply_convert_fusion.1.refs_1_.dout_ref), custom_call_target="tpu_custom_call" | custom-call | tf_op jit(solution)/shard_map/pallas_call | solution.py:143
  138.3 4.5 copy-done.1
  142.8 4.6 copy-done
  147.5 1.0 convert_reduce_fusion
  149.0 3.0 fusion.6
  152.1 5.7 %fusion.4 = f32[256,1536]{0,1:T(8,128)} fusion(bf16[1536,4224]{1,0:T(8,128)(2,1)} %bitcast.57, bf16[256,1536]{0,1:T(8,128)(2,1)S(1)} %copy.67, f32[1536]{0:T(1024)S(1)} %get-tuple-element.67, f32[256]{0:T(256)S(1)} %add_rsqrt_fusion.1), kind=kOutput, calls=%fused_computation.8 | convolution fusion | flops 1209532416 | bytes 7085056 | tf_op jit(solution)/shard_map/dot_general | solution.py:986
  158.4 1.7 subtract_convert_fusion
  160.2 1.0 fusion.19
  161.3 1.9 fusion.35
  164.0 4.6 multiply_reduce_fusion
  168.8 1.6 multiply_convert_fusion
  170.4 2.3 copy.79.x_ref.mixed_ref
  172.7 1.7 fusion.36
  175.9 4.0 pad_maximum_fusion.wgu_ref
  180.5 191.6 %shard_map.213 = (f32[256,1536]{1,0:T(8,128)}, f32[16,8,256]{2,1,0:T(8,128)}, bf16[1536,1024]{1,0:T(8,128)(2,1)}, bf16[512,1536]{1,0:T(8,128)(2,1)}, bf16[8,256,...) custom-call(bf16[256,1536]{1,0:T(8,128)(2,1)} %copy.79.x_ref.mixed_r, ...), custom_call_target="tpu_custom_call" | custom-call | tf_op jit(solution)/shard_map/pallas_call | solution.py:870
  372.2 1.6 collective-permute-start
  374.3 1.6 copy.80.middle_ref
  376.0 0.8 copy.83.k_ref
  376.9 1.2 copy.82.q_ref
  381.2 159.1 %shard_map.214 = (bf16[256,1536]{1,0:T(8,128)(2,1)}, bf16[256,1536]{1,0:T(8,128)(2,1)}, f32[96,4224]{1,0:T(8,128)}) custom-call(bf16[8,256,1536]{2,1,0:T(8,128)(2,1)} %get-tuple-element.24.od_ref, bf16[8,256,1536]{2,1,0:T(8,128)(2,1)} %get-tuple-element.25.sd_ref, bf16[1536,4224]{1,0:T(8,128)(2,1)} %bitcast.60, f32[256,1536]{1,0:T(8,128)} %get-tuple-element.26.dmix_ref, ...), custom_call_target="tpu_custom_call" | custom-call | tf_op jit(solution)/shard_map/pallas_call | solution.py:575
  540.3 1.9 slice.74
  542.2 0.8 slice.77
  543.7 1.6 slice_reduce_fusion
  545.3 2.3 fusion.34
  547.6 3.7 add_bitcast_fusion
  551.3 3.3 convert_add_fusion
  554.6 3.4 slice_bitcast_fusion
  558.1 0.9 copy.97
  559.0 0.9 copy.98
  (99 shorter events, 10.2 us)
Async XLA Ops:
  0.6 147.9 %copy-start.6 = (bf16[256,1536]{1,0:T(8,128)(2,1)S(1)}, bf16[256,1536]{1,0:T(8,128)(2,1)}, u32[]{:S(2)}) copy-start(bf16[256,1536]{1,0:T(8,128)(2,1)} %tokens_ref.1) | copy-start | bytes 2359300
  5.1 143.9 %copy-start.2 = (bf16[256,1536]{1,0:T(8,128)(2,1)}, bf16[256,1536]{1,0:T(8,128)(2,1)S(1)}, u32[]{:S(2)}) copy-start(bf16[256,1536]{1,0:T(8,128)(2,1)S(1)} %multiply_convert_fusion.1.refs_1_.dout_ref) | copy-start | bytes 2359300
  138.3 4.5 copy-start.1
  142.8 4.6 copy-start
  148.5 3.5 copy-start.20
  149.0 3.0 copy-start.28
  157.8 3.4 copy-start.7
  158.3 2.9 copy-start.9
  158.4 2.9 copy-start.11
  160.1 1.2 copy-start.3
  163.9 4.7 copy-start.17
  163.9 4.7 copy-start.27
  164.0 4.8 copy-start.18
  164.0 4.8 copy-start.21
  164.0 4.8 copy-start.29
  174.4 0.7 copy-start.13
  174.4 0.6 copy-start.23
  175.1 0.6 copy-start.25
  372.1 3.8 copy-start.22
  372.2 3.8 copy-start.19
  372.2 3.8 copy-start.10
  372.2 3.8 copy-start.12
  372.2 4.7 copy-start.4
  372.2 179.1 %collective-permute-start = (bf16[1536,1024]{1,0:T(8,128)(2,1)}, bf16[1536,1024]{1,0:T(8,128)(2,1)}, u32[]{:S(2)}, u32[]{:S(2)}) collective-permute-start(bf16[1536,1024]{1,0:T(8,128)(2,1)} %get-tuple-element.31), channel_id=1, source_target_pairs={{0,16},{16,0},{1,17},{17,1},{2,18},{18,2},{3,19},{19,3},{4,20},{20... | collective-permute-start | bytes 9437192 | tf_op jit(solution)/shard_map/ppermute | solution.py:934
  373.8 173.8 %collective-permute-start.1 = (bf16[512,1536]{1,0:T(8,128)(2,1)}, bf16[512,1536]{1,0:T(8,128)(2,1)}, u32[]{:S(2)}, u32[]{:S(2)}) collective-permute-start(bf16[512,1536]{1,0:T(8,128)(2,1)} %get-tuple-element.32), channel_id=1, source_target_pairs={{0,16},{16,0},{1,17},{17,1},{2,18},{18,2},{3,19},{19,3},{4,20},{20... | collective-permute-start | bytes 4718600 | tf_op jit(solution)/shard_map/ppermute | solution.py:934
  375.9 3.7 copy-start.14
  375.9 3.7 copy-start.24
  375.9 3.7 copy-start.26
  540.3 7.3 %copy-start.8 = (bf16[512,1536]{1,0:T(8,128)(2,1)S(1)}, bf16[512,1536]{1,0:T(8,128)(2,1)}, u32[]{:S(2)}) copy-start(bf16[512,1536]{1,0:T(8,128)(2,1)} %get-tuple-element.32) | copy-start | bytes 4718596
  547.6 3.7 copy-start.5
  554.6 3.5 copy-start.16
  554.6 4.3 copy-start.15

commit v2 on v1

--- a/solution.py
+++ b/solution.py
@@ -76,10 +76,44 @@
     return [(edges[i], edges[i + 1] - edges[i]) for i in range(parts)]
 
 
-def gather_kernel(n, cuts, count, *refs):
-    xs, outs, (own_sem, ss, rs, css, crs) = refs[:count], refs[count : 2 * count], refs[2 * count :]
+def forward_kernel(
+    n,
+    wall_ref,
+    dout_ref,
+    tokens_ref,
+    chosen_ref,
+    cos_ref,
+    sin_ref,
+    wallg_ref,
+    doutg_ref,
+    q_ref,
+    k_ref,
+    v_ref,
+    normed_t_ref,
+    attended_t_ref,
+    middle_ref,
+    mixed_ref,
+    gates_ref,
+    gate_rows_ref,
+    gains_ref,
+    weights,
+    out_w,
+    proj,
+    attended,
+    own_sem,
+    load_sem,
+    ss,
+    rs,
+    css,
+    crs,
+):
     place = Place(n)
-    half = place.half
+    half, me = place.half, place.me
+    rows, width = tokens_ref.shape
+    shard = wall_ref.shape[0]
+    q_width, kv_width = q_ref.shape[1], 2 * k_ref.shape[1]
+    qkv_width = q_width + kv_width
+    near = qkv_width + 128
     meet((place.right, place.left, place.sibling))
     started = []
 
@@ -87,75 +121,218 @@
         copy.start()
         started.append(copy)
 
-    def has(d, k, q, parts):
-        return k < half or ((q < parts // 2) == (d == 0))
-
-    for a in range(count):
-        x_ref, o_ref = xs[a], outs[a]
-        parts = len(cuts[a])
-        own = pltpu.make_async_copy(x_ref, o_ref.at[place.me], own_sem.at[a])
-        own.start()
-
-        def part(ref, q, a=a):
-            return ref.at[:, pl.ds(*cuts[a][q])]
-
-        def along(d, k, q, a=a, x_ref=x_ref, o_ref=o_ref):
-            b = place.device(1 - k) if d == 0 else place.device(k - 1)
-            src = part(x_ref, q) if k == 1 else part(o_ref.at[b], q)
-            return remote(
-                src,
-                part(o_ref.at[b], q),
-                ss.at[a, d, k - 1, q],
-                rs.at[a, d, k - 1, q],
-                place.right if d == 0 else place.left,
-            )
-
-        def across(d, k, q, a=a, x_ref=x_ref, o_ref=o_ref):
-            b = place.me if k == 0 else (place.device(-k) if d == 0 else place.device(k))
-            src = part(x_ref, q) if k == 0 else part(o_ref.at[b], q)
-            return remote(src, part(o_ref.at[b], q), css.at[a, d, k, q], crs.at[a, d, k, q], place.sibling)
-
-        for k in range(1, half + 2):
-            for i in range(parts):
-                for d in (0, 1):
-                    q = i if d == 0 else parts - 1 - i
-                    if k > 1 and has(d, k - 1, q, parts):
-                        along(d, k - 1, q).wait_recv()
-                    if k <= half and has(d, k, q, parts):
-                        begin(along(d, k, q))
-                    if k == 1 and d == 0:
-                        begin(across(0, 0, q))
-                    if k > 1 and has(d, k - 1, q, parts):
-                        begin(across(d, k - 1, q))
-        for k in range(half + 1):
-            for q in range(parts):
-                for d in (0, 1):
-                    if (k == 0 and d == 0) or (k > 0 and has(d, k, q, parts)):
-                        across(d, k, q).wait_recv()
-        own.wait()
+    flows = (
+        (wall_ref, wallg_ref, column_cuts(near, 2), weights),
+        (wall_ref, wallg_ref, [(near + s, z) for s, z in column_cuts(width, 2)], out_w),
+        (dout_ref, doutg_ref, column_cuts(width, 2), None),
+    )
+
+    def part(a, ref, q):
+        return ref.at[:, pl.ds(*flows[a][2][q])]
+
+    def block_at(d, k):
+        return me if k == 0 else (place.device(-k) if d == 0 else place.device(k))
+
+    def along(a, d, k, q):
+        x_ref, o_ref = flows[a][:2]
+        b = block_at(d, k - 1)
+        return remote(
+            part(a, x_ref if k == 1 else o_ref.at[b], q),
+            part(a, o_ref.at[b], q),
+            ss.at[a, d, k - 1, q],
+            rs.at[a, d, k - 1, q],
+            place.right if d == 0 else place.left,
+        )
+
+    def across(a, d, k, q):
+        x_ref, o_ref = flows[a][:2]
+        b = block_at(d, k)
+        return remote(
+            part(a, x_ref if k == 0 else o_ref.at[b], q),
+            part(a, o_ref.at[b], q),
+            css.at[a, d, k, q],
+            crs.at[a, d, k, q],
+            place.sibling,
+        )
+
+    def take(a, b, q, src=None):
+        x_ref, o_ref, cuts, local = flows[a]
+        if local is not None:
+            start, size = cuts[q]
+            at = pl.ds(pl.multiple_of(b * shard, 16), shard)
+            pltpu.make_async_copy(
+                part(a, o_ref.at[b] if src is None else src, q),
+                local.at[at, pl.ds(start - cuts[0][0], size)],
+                load_sem.at[a],
+            ).start()
+
+    def first(a):
+        for q in range(2):
+            begin(along(a, 0, 1, q))
+            begin(along(a, 1, 1, 1 - q))
+            begin(across(a, 0, 0, q))
+            take(a, me, q, flows[a][0])
+
+    def sibling_of(b):
+        return b + 1 - 2 * lax.rem(b, 2)
+
+    def met(a, k):
+        for q in range(2):
+            for d in (0, 1):
+                if (k == 0 and d == 0) or (k > 0 and goes(d, k, q, half, 2)):
+                    b = sibling_of(block_at(d, k))
+                    o_ref = flows[a][1]
+                    piece = part(a, o_ref.at[b], q)
+                    remote(piece, piece, css.at[a, d, k, q], crs.at[a, d, k, q], place.sibling).wait_recv()
+                    take(a, b, q)
+
+    def flow():
+        first(0)
+        for a in range(len(flows)):
+            for k in range(2, half + 2):
+                for i in range(2):
+                    for d in (0, 1):
+                        q = i if d == 0 else 1 - i
+                        if goes(d, k - 1, q, half, 2):
+                            along(a, d, k - 1, q).wait_recv()
+                            if k <= half and goes(d, k, q, half, 2):
+                                begin(along(a, d, k, q))
+                            begin(across(a, d, k - 1, q))
+                            take(a, block_at(d, k - 1), q)
+                            yield
+                if k == half and a + 1 < len(flows):
+                    first(a + 1)
+                met(a, k - 2)
+            met(a, half - 0)
+            yield
+
+    per_flow = (half - 1) * 4 + 2 + 1
+    moving = flow()
+    done = [0]
+
+    def pump(steps):
+        while done[0] < steps:
+            next(moving)
+            done[0] += 1
+
+    own = [
+        pltpu.make_async_copy(x_ref, o_ref.at[me], own_sem.at[i])
+        for i, (x_ref, o_ref) in enumerate(((wall_ref, wallg_ref), (dout_ref, doutg_ref)))
+    ]
+    pump(1)
+    for copy in own:
+        copy.start()
+    pump(per_flow)
+    pltpu.make_async_copy(weights, weights, load_sem.at[0]).wait()
+
+    lane = lax.broadcasted_iota(jnp.int32, (rows, 128), 1)
+    turned = jnp.transpose(weights[:, pl.ds(qkv_width, 128)].astype(f32))
+    gains_ref[...] = jnp.concatenate([turned[n : n + 1], turned[n + 1 : n + 2], jnp.zeros((6, width), f32)], axis=0)
+    inputs = tokens_ref[...].astype(f32)
+    inv = lax.rsqrt(jnp.mean(inputs * inputs, axis=1, keepdims=True) + EPSILON)
+    normed = (inputs * inv * gains_ref[0:1]).astype(bf16)
+    proj[...] = mul(normed, weights[:, pl.ds(0, qkv_width)], 1, 0)
+    normed_t_ref[...] = jnp.transpose(normed)
+    cosine, sine = cos_ref[...], sin_ref[...]
+    sine_on = jnp.where(lane % HD < HD // 2, -sine, sine)
+
+    def turn(at):
+        block = proj[:, at]
+        return (block * cosine + swap_halves(block, lane) * sine_on).astype(bf16)
+
+    for b in range(q_width // 128):
+        q_ref[:, pl.ds(128 * b, 128)] = turn(pl.ds(128 * b, 128))
+    for b in range(kv_width // 256):
+        k_ref[:, pl.ds(128 * b, 128)] = turn(pl.ds(q_width + 128 * b, 128))
+    v_ref[...] = proj[:, pl.ds(q_width + kv_width // 2, kv_width // 2)].astype(bf16)
+    t_at = lax.broadcasted_iota(jnp.int32, (rows, rows), 0)
+    u_at = lax.broadcasted_iota(jnp.int32, (rows, rows), 1)
+    causal = t_at >= u_at
+    kv_count = k_ref.shape[1] // HD
+    per_group = q_width // HD // kv_count
+    kept = None
+    for g in range(kv_count):
+        pair = pl.ds(128 * (g // 2), 128)
+        k_parts = head_halves(k_ref[:, pair].astype(f32), lane, g % 2)
+        v_parts = head_halves(v_ref[:, pair].astype(f32), lane, g % 2)
+        for h in range(per_group * g, per_group * (g + 1)):
+            at = pl.ds(128 * (h // 2), 128)
+            probs = softmax_rows(q_ref[:, at], k_parts[h % 2], causal).astype(bf16)
+            kept_new = mul(probs, v_parts[h % 2], 1, 0)
+            if h % 2 == 0:
+                kept = kept_new
+            else:
+                attended[:, at] = (kept + kept_new).astype(bf16)
+        pump(per_flow + per_flow * (g + 1) // kv_count)
+    attended_t_ref[...] = jnp.transpose(attended[...])
+    pltpu.make_async_copy(out_w, out_w, load_sem.at[1]).wait()
+    middle_ref[...] = tokens_ref[...].astype(f32) + mul(attended[...], out_w[...], 1, 0)
+    tile = 32
+
+    @pl.loop(0, rows // tile)
+    def _(r):
+        at = pl.ds(pl.multiple_of(r * tile, tile), tile)
+        middle = middle_ref[at]
+        scale = lax.rsqrt(jnp.mean(middle * middle, axis=1, keepdims=True) + EPSILON)
+        mixed_ref[at] = (middle * scale * gains_ref[1:2]).astype(bf16)
+
+    logits = mul(mixed_ref[...], weights[:, pl.ds(qkv_width, 128)], 1, 0)
+    chosen = chosen_ref[...] > 0
+    logits = jnp.where(chosen, logits, -1e30)
+    e = jnp.where(chosen, jnp.exp(logits - jnp.max(logits, axis=1, keepdims=True)), 0.0)
+    gates = e / jnp.sum(e, axis=1, keepdims=True)
+    gates_ref[...] = gates
+    across_gates = jnp.transpose(gates)
+    for e in range(n):
+        gate_rows_ref[e] = jnp.broadcast_to(across_gates[e : e + 1], (8, rows))
+    for _ in moving:
+        pass
+    for copy in own:
+        copy.wait()
     for copy in started:
         copy.wait_send()
 
 
-def gather(n, arrays, collective_id):
-    half, count = n // 4, len(arrays)
-    cuts = [column_cuts(x.shape[1], 2) for x in arrays]
+def forward(n, wall, d_out, tokens, chosen, turns, q_width, kv_width, collective_id):
+    half = n // 4
+    rows, width = tokens.shape
+    shard, full_width = wall.shape
+    near = q_width + kv_width + 128
+    shape = jax.ShapeDtypeStruct
     return pl.pallas_call(
-        functools.partial(gather_kernel, n, cuts, count),
-        out_shape=[jax.ShapeDtypeStruct((n,) + x.shape, x.dtype) for x in arrays],
-        in_specs=[ANY] * count,
-        out_specs=[ANY] * count,
+        functools.partial(forward_kernel, n),
+        out_shape=[
+            shape((n, shard, full_width), bf16),
+            shape((n, rows, width), bf16),
+            shape((rows, q_width), bf16),
+            shape((rows, kv_width // 2), bf16),
+            shape((rows, kv_width // 2), bf16),
+            shape((width, rows), bf16),
+            shape((q_width, rows), bf16),
+            shape((rows, width), f32),
+            shape((rows, width), bf16),
+            shape((rows, 128), f32),
+            shape((n, 8, rows), f32),
+            shape((8, width), f32),
+        ],
+        in_specs=[ANY] * 2 + [VMEM] * 4,
+        out_specs=[ANY] * 2 + [VMEM] * 10,
         scratch_shapes=[
-            DMA((count,)),
-            DMA((count, 2, half, 2)),
-            DMA((count, 2, half, 2)),
-            DMA((count, 2, half + 1, 2)),
-            DMA((count, 2, half + 1, 2)),
+            pltpu.VMEM((width, near), bf16),
+            pltpu.VMEM((q_width, width), bf16),
+            pltpu.VMEM((rows, q_width + kv_width), f32),
+            pltpu.VMEM((rows, q_width), bf16),
+            DMA((2,)),
+            DMA((2,)),
+            DMA((3, 2, half, 2)),
+            DMA((3, 2, half, 2)),
+            DMA((3, 2, half + 1, 2)),
+            DMA((3, 2, half + 1, 2)),
         ],
         compiler_params=pltpu.CompilerParams(
-            collective_id=collective_id, has_side_effects=True, vmem_limit_bytes=16 * MB
+            collective_id=collective_id, has_side_effects=True, vmem_limit_bytes=56 * MB
         ),
-    )(*arrays)
+    )(wall, d_out, tokens, chosen, *turns)
 
 
 SLOTS = 4
@@ -359,9 +536,9 @@
     for turn in range(1, dp):
         pl.semaphore_signal(barrier, inc=1, device_id={"dp": lax.rem(rank + turn, dp)}, device_id_type=MESH)
     out_w = pltpu.make_async_copy(
-        wall_ref.at[:, pl.ds(qkv_width, width)], weights.at[:, pl.ds(0, width)], weight_sem.at[0]
+        wall_ref.at[:, pl.ds(qkv_width + 128, width)], weights.at[:, pl.ds(0, width)], weight_sem.at[0]
     )
-    extra_copy = pltpu.make_async_copy(wall_ref.at[:, pl.ds(qkv_width + width, 128)], extra_w, weight_sem.at[1])
+    extra_copy = pltpu.make_async_copy(wall_ref.at[:, pl.ds(qkv_width, 128)], extra_w, weight_sem.at[1])
     qkv_w = pltpu.make_async_copy(wall_ref.at[:, pl.ds(0, qkv_width)], weights, weight_sem.at[2])
     out_w.start()
     extra_copy.start()
@@ -487,8 +664,8 @@
     def fill(ref, device):
         at = pl.ds(pl.multiple_of(device * shard, 16), shard)
         ref[:, pl.ds(0, qkv_width)] = mul(normed_t_ref[at], d_qkv[...], 1, 0).astype(bf16)
-        ref[:, pl.ds(qkv_width, width)] = mul(attended_t_ref[at], d_middle_low[...], 1, 0).astype(bf16)
-        ref[:, pl.ds(qkv_width + width, 128)] = extra[at].astype(bf16)
+        ref[:, pl.ds(qkv_width, 128)] = extra[at].astype(bf16)
+        ref[:, pl.ds(qkv_width + 128, width)] = mul(attended_t_ref[at], d_middle_low[...], 1, 0).astype(bf16)
 
     @pl.loop(0, ring)
     def _(i):
@@ -630,6 +807,7 @@
     oe_ref,
     se_ref,
     xg_ref,
+    hg_ref,
     acc_gu,
     acc_d,
     gate_in,
@@ -638,6 +816,7 @@
     dobuf,
     pd,
     pe,
+    hbuf,
     own_sem,
     ring_s,
     ring_r,
@@ -659,8 +838,7 @@
     piece = rows // QUARTERS
     meet_all(place)
 
-    own = pltpu.make_async_copy(x_ref, xg_ref.at[me], own_sem.at[0])
-    own.start()
+    own = pltpu.make_async_copy(xbuf.at[0], xg_ref.at[me], own_sem.at[0])
 
     def at(q):
         return pl.ds(pl.multiple_of(q * piece, piece), piece)
@@ -668,34 +846,34 @@
     def block_of(d, k):
         return jnp.where(d == 0, place.device(-k), place.device(k))
 
-    def along(d, k, q):
-        b = block_of(d, k - 1)
+    def along(d, k, q, first=False):
+        b = me if first else block_of(d, k - 1)
         return remote(
-            xg_ref.at[b, at(q)],
+            x_ref.at[at(q)] if first else xg_ref.at[b, at(q)],
             xg_ref.at[b, at(q)],
             ring_s.at[d, k - 1, q],
             ring_r.at[d, k - 1, q],
             jnp.where(d == 0, place.right, place.left),
         )
 
-    def across(d, k, q):
-        b = block_of(d, k)
-        return remote(xg_ref.at[b, at(q)], xg_ref.at[b, at(q)], cross_s.at[d, k, q], cross_r.at[d, k, q], place.sibling)
+    def across(d, k, q, first=False):
+        b = me if first else block_of(d, k)
+        src = x_ref.at[at(q)] if first else xg_ref.at[b, at(q)]
+        return remote(src, xg_ref.at[b, at(q)], cross_s.at[d, k, q], cross_r.at[d, k, q], place.sibling)
 
     def gate_copy(d):
         to = lax.rem(me + d, n)
         return remote(gates_ref.at[to], gate_in.at[me], gate_s.at[d], gate_r.at[d], to)
 
+    for q in range(QUARTERS):
+        for d in (0, 1):
+            along(d, 1, q, first=True).start()
+        across(0, 0, q, first=True).start()
+
     @pl.loop(1, n)
     def _(d):
         gate_copy(d).start()
 
-    own.wait()
-    for q in range(QUARTERS):
-        for d in (0, 1):
-            along(d, 1, q).start()
-    for q in range(QUARTERS):
-        across(0, 0, q).start()
     gate_in[me] = gates_ref[me]
     acc_gu[...] = jnp.zeros_like(acc_gu)
     acc_d[...] = jnp.zeros_like(acc_d)
@@ -728,15 +906,22 @@
         )
 
     def put_wait(slot):
-        for which, buf in enumerate((pd, pe)):
+        for which, buf in enumerate((pd, pe, hbuf)):
             pltpu.make_async_copy(buf.at[slot], buf.at[slot], put_sem.at[which, slot]).wait()
 
     def dgate_copy(block):
         d = lax.rem(block - me + n, n)
         return remote(dgate_out.at[block], dgates_ref.at[me], dgate_s.at[d], dgate_r.at[d], block)
 
-    for copy in load(me, 0):
-        copy.start()
+    def load_rest(block, slot):
+        return (
+            pltpu.make_async_copy(xg_ref.at[block], xbuf.at[slot], load_sem.at[0, slot]),
+            pltpu.make_async_copy(dog_ref.at[block], dobuf.at[slot], load_sem.at[1, slot]),
+            pltpu.make_async_copy(hg_ref.at[block], hbuf.at[slot], load_sem.at[2, slot]),
+        )
+
+    pltpu.make_async_copy(x_ref, xbuf.at[0], load_sem.at[0, 0]).start()
+    pltpu.make_async_copy(dog_ref.at[me], dobuf.at[0], load_sem.at[1, 0]).start()
 
     @pl.loop(0, n)
     def _(i):
@@ -744,6 +929,10 @@
         slot = lax.rem(i, 2)
         for copy in load(block, slot):
             copy.wait()
+
+        @pl.when(i == 0)
+        def _():
+            own.start()
 
         @pl.when(i > 0)
         def _():
@@ -791,6 +980,10 @@
                     xg_ref.at[b, at(q)], xg_ref.at[b, at(q)], cross_s.at[dd, nk, q], cross_r.at[dd, nk, q], place.sibling
                 ).wait_recv()
 
+        @pl.when(i == 0)
+        def _():
+            own.wait()
+
         @pl.when(i + 1 < n)
         def _():
             for copy in load(nblock, 1 - slot):
@@ -804,6 +997,8 @@
         d_g = (dh * u * s * (1.0 + g * (1.0 - s))).astype(bf16)
         d_u = (dh * gs).astype(bf16)
         dgu = jnp.concatenate([d_g, d_u], axis=1)
+        hbuf[slot] = jnp.concatenate([d_g, d_u, hidg], axis=1)
+        pltpu.make_async_copy(hbuf.at[slot], hg_ref.at[block], put_sem.at[2, slot]).start()
         pe[slot] = mul(dgu, wgu_ref[...], 1, 1).astype(bf16)
 
         @pl.when(i > 0)
@@ -824,24 +1019,45 @@
             remote(pd.at[slot], sd_ref.at[chip], put_sem.at[0, slot], sib_r.at[0, chip], place.sibling).start()
             remote(pe.at[slot], se_ref.at[chip], put_sem.at[1, slot], sib_r.at[1, chip], place.sibling).start()
 
-        acc_gu[...] += mul(x, dgu, 0, 0)
-        acc_d[...] += mul(hidg, do, 0, 0)
-
     put_wait(0)
     put_wait(1)
+
+    def other_wait(chip):
+        remote(se_ref.at[chip], se_ref.at[chip], put_sem.at[1, 0], sib_r.at[1, chip], place.sibling).wait_recv()
+
+    def write(at, columns, total):
+        de_ref[at, columns] = total
+
+    for copy in load_rest(0, 0):
+        copy.start()
+
+    def gradients(first, last):
+        @pl.loop(first, last)
+        def _(b):
+            slot = lax.rem(b, 2)
+            for copy in load_rest(b, slot):
+                copy.wait()
+
+            @pl.when(b + 1 < n)
+            def _():
+                for copy in load_rest(b + 1, 1 - slot):
+                    copy.start()
+
+            acc_gu[...] += mul(xbuf[slot], hbuf[slot, :, pl.ds(0, 2 * hidden_width)], 0, 0)
+            acc_d[...] += mul(hbuf[slot, :, pl.ds(2 * hidden_width, hidden_width)], dobuf[slot], 0, 0)
+
+    steps = len(ring_work(half, 2)) // 2
+    back = ring_reduce(
+        place, lambda chip: oe_ref.at[chip], lambda chip: se_ref.at[chip], other_wait, width, write, reduce_refs
+    )
+    for step in range(steps):
+        next(back)
+        next(back)
+        gradients(n * step // steps, n * (step + 1) // steps)
+    for _ in back:
+        pass
     ggu_ref[...] = acc_gu[...].astype(bf16)
     gd_ref[...] = acc_d[...].astype(bf16)
-
-    def other_wait(chip):
-        remote(se_ref.at[chip], se_ref.at[chip], put_sem.at[1, 0], sib_r.at[1, chip], place.sibling).wait_recv()
-
-    def write(at, columns, total):
-        de_ref[at, columns] = total
-
-    for _ in ring_reduce(
-        place, lambda chip: oe_ref.at[chip], lambda chip: se_ref.at[chip], other_wait, width, write, reduce_refs
-    ):
-        pass
 
     @pl.loop(0, ring)
     def _(chip):
@@ -854,7 +1070,7 @@
         remote(dgates_ref.at[source], dgates_ref.at[source], dgate_s.at[d], dgate_r.at[d], place.sibling).wait()
 
     for q in range(QUARTERS):
-        across(0, 0, q).wait_send()
+        across(0, 0, q, first=True).wait_send()
         for d in (0, 1):
             for k in range(1, half + 1):
                 if k < half or ((q < QUARTERS // 2) == (d == 0)):
@@ -879,9 +1095,10 @@
             blocks,
             blocks,
             jax.ShapeDtypeStruct((n, rows, width), bf16),
+            jax.ShapeDtypeStruct((n, rows, 3 * hidden_width), bf16),
         ],
         in_specs=[ANY, ANY, VMEM, VMEM, VMEM],
-        out_specs=[VMEM, VMEM, VMEM, VMEM, ANY, ANY, ANY, ANY, ANY],
+        out_specs=[VMEM, VMEM, VMEM, VMEM, ANY, ANY, ANY, ANY, ANY, ANY],
         scratch_shapes=[
             pltpu.VMEM(wgu.shape, f32),
             pltpu.VMEM(wd.shape, f32),
@@ -891,13 +1108,14 @@
             pltpu.VMEM((2, rows, width), bf16),
             pltpu.VMEM((2, rows, width), bf16),
             pltpu.VMEM((2, rows, width), bf16),
+            pltpu.VMEM((2, rows, 3 * hidden_width), bf16),
             DMA((1,)),
             DMA((2, half, QUARTERS)),
             DMA((2, half, QUARTERS)),
             DMA((2, half + 1, QUARTERS)),
             DMA((2, half + 1, QUARTERS)),
-            DMA((2, 2)),
-            DMA((2, 2)),
+            DMA((3, 2)),
+            DMA((3, 2)),
             DMA((2, ring)),
             DMA((n,)),
             DMA((n,)),
@@ -910,15 +1128,6 @@
         ),
     )(mixed_in, d_gathered, gate_rows, wgu, wd)
     return out[:6]
-
-
-def rotate(values, cosine, sines):
-    half_dim = values.shape[-1] // 2
-    first_half = values[..., :half_dim]
-    second_half = values[..., half_dim:]
-    return jnp.concatenate(
-        [first_half * cosine - second_half * sines, second_half * cosine + first_half * sines], -1
-    )
 
 
 def rope_tables(length, head_dim):
@@ -956,10 +1165,7 @@
     expert_count = w_router.shape[1]
     head_dim = HD
     kv_width, q_width = w_kv.shape[1], w_query.shape[1]
-    kv_count = kv_width // (2 * head_dim)
-    head_count = q_width // head_dim
-    per_group = head_count // kv_count
-    score_scale = head_dim ** (-0.5)
+    qkv_width = q_width + kv_width
     shard = w_query.shape[0]
     live = (jnp.arange(tok_rows) < lengths[0]).astype(f32)
     d_out_low = (cotangent.astype(f32) * live[:, None]).astype(bf16)
@@ -972,64 +1178,19 @@
         ],
         axis=1,
     )
-    wall, d_gathered = gather(n, [jnp.concatenate([w_query, w_kv, w_out, extra], axis=1), d_out_low], 0)
+    chosen = jnp.any(routes[:, :, None] == jnp.arange(128)[None, None, :], axis=1).astype(f32)
+    cosine, sines = rope_tables(tok_rows, head_dim)
+    turns = [jnp.tile(table.reshape(tok_rows, -1), (1, 4)) for table in (cosine, sines)]
+    wall = jnp.concatenate([w_query, w_kv, extra, w_out], axis=1)
+    (wall, d_gathered, queries, keys, values, normed_t, attended_t, middle, mixed_in, gates, gate_rows, gains) = forward(
+        n, wall, d_out_low, tokens, chosen, turns, q_width, kv_width, 0
+    )
     wall = wall.reshape(-1, wall.shape[-1])
-    edges = [0, q_width, q_width + kv_width, q_width + kv_width + model_width]
-    query_w, kv_w, out_w = (wall[:, a:b] for a, b in zip(edges[:-1], edges[1:]))
-    router_w = wall[:, edges[3] : edges[3] + expert_count]
-    gain_one = wall[:, edges[3] + expert_count].astype(f32)
-    gain_two = wall[:, edges[3] + expert_count + 1].astype(f32)
-
-    inputs = tokens.astype(f32)
-    inv_one = lax.rsqrt(jnp.mean(inputs * inputs, axis=-1, keepdims=True) + EPSILON)
-    normed_one = (inputs * inv_one * gain_one).astype(bf16)
-    query_proj = jnp.dot(normed_one, query_w, preferred_element_type=f32)
-    kv_proj = jnp.dot(normed_one, kv_w, preferred_element_type=f32)
-    cosine, sines = rope_tables(tok_rows, head_dim)
-    queries = (
-        rotate(query_proj.reshape(tok_rows, head_count, head_dim), cosine, sines)
-        .astype(bf16)
-        .reshape(tok_rows, kv_count, per_group, head_dim)
-    )
-    keys = rotate(
-        kv_proj[:, : kv_count * head_dim].reshape(tok_rows, kv_count, head_dim), cosine, sines
-    ).astype(bf16)
-    values = kv_proj[:, kv_count * head_dim :].reshape(tok_rows, kv_count, head_dim).astype(bf16)
-    causal = jnp.arange(tok_rows)[:, None] >= jnp.arange(tok_rows)[None, :]
-
-    def masked_scores():
-        scores = (
-            jnp.einsum("tgjd,ugd->gjtu", queries, keys, preferred_element_type=f32) * score_scale
-        )
-        return jnp.where(causal[None, None], scores, -1e30)
-
-    masked = masked_scores()
-    row_peak = jnp.max(masked, axis=-1, keepdims=True)
-    exp_scores = jnp.exp(masked - row_peak)
-    row_total = jnp.sum(exp_scores, axis=-1, keepdims=True)
-    probs_low = (exp_scores / row_total).astype(bf16)
-    attended = (
-        jnp.einsum("gjtu,ugd->tgjd", probs_low, values, preferred_element_type=f32)
-        .astype(bf16)
-        .reshape(tok_rows, head_count * head_dim)
-    )
-    middle = inputs + jnp.dot(attended, out_w, preferred_element_type=f32)
-    inv_two = lax.rsqrt(jnp.mean(middle * middle, axis=-1, keepdims=True) + EPSILON)
-    mixed_in = (middle * inv_two * gain_two).astype(bf16)
-    logits = jnp.dot(mixed_in, router_w, preferred_element_type=f32)
-    chosen = jnp.any(routes[:, :, None] == jnp.arange(expert_count)[None, None, :], axis=1)
-    chosen_logits = jnp.where(chosen, logits, -jnp.inf)
-    weights = jnp.exp(chosen_logits - jnp.max(chosen_logits, axis=-1, keepdims=True))
-    gates = weights / jnp.sum(weights, axis=-1, keepdims=True)
-
-    gate_rows = jnp.broadcast_to(gates.T[:, None, :], (expert_count, 8, tok_rows))
     wgu = jnp.concatenate([expert_gate[0], expert_up[0]], axis=1)
     d_mixed_experts, d_gate_rows, grad_gu, grad_down, own_d, other_d = experts(
         n, mixed_in, d_gathered, gate_rows, wgu, expert_down[0], 1
     )
 
-    turns = [jnp.tile(table.reshape(tok_rows, -1), (1, 4)) for table in (cosine, sines)]
-    gains = jnp.concatenate([gain_one[None], gain_two[None], jnp.zeros((6, model_width), f32)])
     output, input_grad, dense_sum = backward(
         n,
         dp,
@@ -1039,16 +1200,16 @@
         (
             d_mixed_experts,
             d_gate_rows,
-            jnp.pad(gates, ((0, 0), (0, 128 - expert_count))),
+            gates,
             middle,
             mixed_in,
             d_out_low,
             tokens,
-            normed_one.T,
-            attended.T,
-            queries.reshape(tok_rows, -1),
-            keys.reshape(tok_rows, -1),
-            values.reshape(tok_rows, -1),
+            normed_t,
+            attended_t,
+            queries,
+            keys,
+            values,
             *turns,
             gains,
         ),
@@ -1060,12 +1221,12 @@
     return (
         output,
         input_grad,
-        dense_sum[:, edges[3] + expert_count],
-        dense_sum[:, : edges[1]],
-        dense_sum[:, edges[1] : edges[2]],
-        dense_sum[:, edges[2] : edges[3]],
-        dense_sum[:, edges[3] + expert_count + 1],
-        dense_sum[:, edges[3] : edges[3] + expert_count],
+        dense_sum[:, qkv_width + expert_count],
+        dense_sum[:, :q_width],
+        dense_sum[:, q_width:qkv_width],
+        dense_sum[:, qkv_width + 128 :],
+        dense_sum[:, qkv_width + expert_count + 1],
+        dense_sum[:, qkv_width : qkv_width + expert_count],
         grad_gu[None, :, :hidden_width],
         grad_gu[None, :, hidden_width:],
         grad_down[None],

time: 567 us -> 503 us (0.89)
  Pallas kernels: 482 us -> 457 us
  local copies, waits for them, and re-layouts: 36.4 us -> 18.3 us
  matrix products: 16.7 us -> 0 us
  other arithmetic: 20.4 us -> 14.2 us
    pallas_call x1, Pallas kernels: 192 us -> 162 us  [experts(): pl.pallas_call(functools.partial(expert_kernel, n), out_shape=[jax.ShapeD...]
    dot_general x6 -> x0, matrix products: 16.7 us -> none  [the longest x1 5.67 us: per_device(): query_proj = jnp.dot(normed_one, query_w, preferred_element_type=f32)]
    unnamed x65 -> x21, local copies, waits for them, and re-layouts: 13.8 us -> 4.07 us
  transfers between devices with their start and end apart: 2 -> 2, of which waited for: 0 -> 0; matrix products, arithmetic and copies ran while one was open for 3% -> 2% of each run, Pallas kernels for 28% -> 32%
where the time goes in v2:
time: 503 us; the launch traced here: 493 us
  Pallas kernels  457 us (91%)
  local copies, waits for them, and re-layouts  18.3 us (4%)
  other arithmetic  14.2 us (3%)
    pallas_call x1, Pallas kernels, experts(): pl.pallas_call(functools.partial(expert_kernel, n), out_shape=[jax.ShapeD...  162 us
    pallas_call x1, Pallas kernels, backward(): pl.pallas_call(functools.partial(backward_kernel, n, dp), out_shape=[jax....  158 us
    pallas_call x1, Pallas kernels, forward(): pl.pallas_call(functools.partial(forward_kernel, n), out_shape=[shape((n,...  136 us
  transfers between devices with their start and end apart: 2, of which 0 were waited for; matrix products, arithmetic and copies ran while one was open for 2% of the time, Pallas kernels for 32%

profile of v2, /device:TPU:0, one launch (start us, length us, event | category | flops | bytes accessed | tf_op | source)
XLA Modules:
  0.0 493.0 jit_solution(10484091905492871766)
XLA Ops:
  0.6 0.0 copy-start.1
  1.4 0.8 copy.39
  2.2 0.8 copy.40
  3.0 0.8 copy.38
  3.8 0.2 multiply_sine_fusion
  4.0 0.8 copy.43.sin_ref
  4.8 0.8 copy.42.cos_ref
  5.5 0.8 copy.41
  6.4 0.4 fusion
  6.8 0.7 convert_element_type.57.chosen_ref
  7.5 2.2 multiply_convert_fusion.dout_ref
  9.7 0.0 copy-done.1
  9.7 3.6 pad_maximum_fusion.wgu_ref
  13.4 1.1 concatenate.6.wall_ref
  14.4 136.5 %shard_map.212 = (bf16[16,96,4224]{2,1,0:T(8,128)(2,1)}, bf16[16,256,1536]{2,1,0:T(8,128)(2,1)}, bf16[256,1536]{1,0:T(8,128)(2,1)}, bf16[256,512]{1,0:T(8,128)(2...) custom-call(bf16[96,4224]{1,0:T(8,128)(2,1)} %concatenate.6.wall_ref, ...), custom_call_target="tpu_custom_call" | custom-call | tf_op jit(solution)/shard_map/pallas_call | solution.py:302
  150.9 161.5 %shard_map.213 = (f32[256,1536]{1,0:T(8,128)}, f32[16,8,256]{2,1,0:T(8,128)}, bf16[1536,1024]{1,0:T(8,128)(2,1)}, bf16[512,1536]{1,0:T(8,128)(2,1)}, bf16[8,256,...) custom-call(bf16[256,1536]{1,0:T(8,128)(2,1)} %get-tuple-element.32., ...), custom_call_target="tpu_custom_call" | custom-call | tf_op jit(solution)/shard_map/pallas_call | solution.py:1086
  312.5 1.6 collective-permute-start
  314.0 0.5 collective-permute-start.1
  314.6 158.5 %shard_map.214 = (bf16[256,1536]{1,0:T(8,128)(2,1)}, bf16[256,1536]{1,0:T(8,128)(2,1)}, f32[96,4224]{1,0:T(8,128)}) custom-call(bf16[8,256,1536]{2,1,0:T(8,128)(2,1)} %get-tuple-element.35.od_ref, bf16[8,256,1536]{2,1,0:T(8,128)(2,1)} %get-tuple-element.36.sd_ref, bf16[1536,4224]{1,0:T(8,128)(2,1)} %bitcast.16, f32[256,1536]{1,0:T(8,128)} %get-tuple-element.38.dmix_ref, ...), custom_call_target="tpu_custom_call" | custom-call | tf_op jit(solution)/shard_map/pallas_call | solution.py:752
  473.1 0.9 slice.29
  474.0 1.8 slice.26
  475.8 0.7 copy.46
  476.4 1.6 slice_reduce_fusion
  478.0 2.3 fusion.1
  480.3 0.0 collective-permute-done.1
  480.4 3.7 add_bitcast_fusion
  484.0 0.0 collective-permute-done
  484.0 3.3 convert_add_fusion
  487.4 3.4 slice_bitcast_fusion
  490.8 0.9 copy.50
  491.7 0.0 copy-done.3
  491.7 0.9 copy.51
  (19 shorter events, 0.1 us)
Async XLA Ops:
  0.6 9.0 %copy-start.1 = (bf16[1,1536,512]{2,1,0:T(8,128)(2,1)S(1)}, bf16[1,1536,512]{2,1,0:T(8,128)(2,1)}, u32[]{:S(2)}) copy-start(bf16[1,1536,512]{2,1,0:T(8,128)(2,1)} %param.24) | copy-start | bytes 4718596
  9.7 3.7 copy-start.5
  9.7 3.7 copy-start.6
  9.7 3.7 copy-start.7
  312.5 171.6 %collective-permute-start = (bf16[1536,1024]{1,0:T(8,128)(2,1)}, bf16[1536,1024]{1,0:T(8,128)(2,1)}, u32[]{:S(2)}, u32[]{:S(2)}) collective-permute-start(bf16[1536,1024]{1,0:T(8,128)(2,1)} %get-tuple-element.51), channel_id=1, source_target_pairs={{0,16},{16,0},{1,17},{17,1},{2,18},{18,2},{3,19},{19,3},{4,20},{20... | collective-permute-start | bytes 9437192 | tf_op jit(solution)/shard_map/ppermute | solution.py:1143
  314.0 166.3 %collective-permute-start.1 = (bf16[512,1536]{1,0:T(8,128)(2,1)}, bf16[512,1536]{1,0:T(8,128)(2,1)}, u32[]{:S(2)}, u32[]{:S(2)}) collective-permute-start(bf16[512,1536]{1,0:T(8,128)(2,1)} %get-tuple-element.52), channel_id=1, source_target_pairs={{0,16},{16,0},{1,17},{17,1},{2,18},{18,2},{3,19},{19,3},{4,20},{20... | collective-permute-start | bytes 4718600 | tf_op jit(solution)/shard_map/ppermute | solution.py:1143
  473.1 7.3 %copy-start.2 = (bf16[512,1536]{1,0:T(8,128)(2,1)S(1)}, bf16[512,1536]{1,0:T(8,128)(2,1)}, u32[]{:S(2)}) copy-start(bf16[512,1536]{1,0:T(8,128)(2,1)} %get-tuple-element.52) | copy-start | bytes 4718596
  480.3 3.7 copy-start
  487.4 3.5 copy-start.4
  487.4 4.3 copy-start.3
